TPU v7x, 32 devices: a whole 2x2x4 slice. The times are simulated.
32 devices in a mesh: grp: 4 (over y, core), wide: 4 (over z), tp: 2 (over x).
Axes of the slice: x: 2, y: 2, z: 4, core: 2. Of those that a mesh axis runs over, the one named last changes fastest.
Arguments:
- layer_input: bfloat16 [4096, 768], P(('grp', 'wide')), may hold values from -6 to 6
- memory: bfloat16 [4096, 768], P(('grp', 'wide')), may hold values from -6 to 6
- reader_map: int32 [4096], P('grp'), may hold values from 0 to 3, as said below
- target_ids: int32 [4096], P('grp'), may hold values from 0 to 32127
- target_lengths: int32 [16], replicated, may hold values from 128 to 256, as said below
- out_grad: bfloat16 [4096, 768], P(('grp', 'wide')), may hold values from -0.00036621094 to 0.00036621094
- self_q: bfloat16 [768, 768], P('wide', 'tp'), may hold values from -0.21875 to 0.21875
- self_k: bfloat16 [768, 768], P('wide', 'tp'), may hold values from -0.21875 to 0.21875
- self_v: bfloat16 [768, 768], P('wide', 'tp'), may hold values from -0.21875 to 0.21875
- self_o: bfloat16 [768, 768], P('wide', 'tp'), may hold values from -0.75 to 0.75
- cross_q: bfloat16 [768, 768], P('wide', 'tp'), may hold values from -0.21875 to 0.21875
- cross_k: bfloat16 [768, 768], P('wide', 'tp'), may hold values from -0.21875 to 0.21875
- cross_v: bfloat16 [768, 768], P('wide', 'tp'), may hold values from -0.21875 to 0.21875
- cross_o: bfloat16 [768, 768], P('wide', 'tp'), may hold values from -0.75 to 0.75
- ff_gate: bfloat16 [768, 2048], P('wide', 'tp'), may hold values from -0.21875 to 0.21875
- ff_up: bfloat16 [768, 2048], P('wide', 'tp'), may hold values from -0.21875 to 0.21875
- ff_out: bfloat16 [768, 2048], P('wide', 'tp'), may hold values from -0.125 to 0.125
- gain_self: bfloat16 [768], P('wide'), may hold values from 0.099609375 to 1.8984375
- gain_cross: bfloat16 [768], P('wide'), may hold values from 0.099609375 to 1.8984375
- gain_ff: bfloat16 [768], P('wide'), may hold values from 0.099609375 to 1.8984375
- gain_exit: bfloat16 [768], P('wide'), may hold values from 0.099609375 to 1.8984375
- exit_table: bfloat16 [32128, 768], P(('wide', 'tp')), may hold values from -9 to 9
Outputs:
- block_output: bfloat16 [4096, 768], P(('grp', 'wide'))
- loss: float32 [], replicated
- input_grad: float32 [4096, 768], P(('grp', 'wide'))
- memory_grad: float32 [4096, 768], P(('grp', 'wide'))
- self_q_grad: float32 [768, 768], P('wide', 'tp')
- self_k_grad: float32 [768, 768], P('wide', 'tp')
- self_v_grad: float32 [768, 768], P('wide', 'tp')
- self_o_grad: float32 [768, 768], P('wide', 'tp')
- cross_q_grad: float32 [768, 768], P('wide', 'tp')
- cross_k_grad: float32 [768, 768], P('wide', 'tp')
- cross_v_grad: float32 [768, 768], P('wide', 'tp')
- cross_o_grad: float32 [768, 768], P('wide', 'tp')
- ff_gate_grad: float32 [768, 2048], P('wide', 'tp')
- ff_up_grad: float32 [768, 2048], P('wide', 'tp')
- ff_out_grad: float32 [768, 2048], P('wide', 'tp')
- gain_self_grad: float32 [768], P('wide')
- gain_cross_grad: float32 [768], P('wide')
- gain_ff_grad: float32 [768], P('wide')
- gain_exit_grad: float32 [768], P('wide')
- exit_grad: float32 [32128, 768], P(('wide', 'tp'))
Inputs may be any that keep to these rules, and one draw needn't show every extreme that they name: `reader_map`: each memory row is read by exactly one target sequence of its group; every sequence reads at least one row of its group; of the 256 rows held by one device, at most 128 are read by one sequence, and in each group one sequence reads exactly 128 rows held on every device of wide. `target_lengths`: some sequence has the full length 256.
All inputs are finite; a program needn't handle non-finite values.
Results may differ from a plain program's by a relative error of at most 0.03.
Values may be sent and summed in bfloat16 or wider, within the bound.
A program may use at most 192 MiB of HBM per device.

v0:
```python
import jax
import jax.numpy as jnp
from jax import lax
from jax.sharding import PartitionSpec as P

HEAD_DIM = 64


EPSILON = 1e-06
MASKED = -1e30


def merged(shard, axis, combine):
    everything = jax.tree.map(
        lambda part, kind: lax.all_gather(part.astype(kind), axis),
        shard,
        (jnp.bfloat16, jnp.bfloat16, jnp.bfloat16),
    )

    def take(k):
        return jax.tree.map(lambda part, own: part[k].astype(own.dtype), everything, shard)

    return lax.fori_loop(
        1, lax.axis_size(axis), lambda k, so_far: combine(so_far, take(k)), take(0)
    )


def project(left, right):
    return jnp.dot(left, right, preferred_element_type=jnp.float32)


def project_back(left, right):
    return lax.dot_general(
        left, right, (((1,), (1,)), ((), ())), preferred_element_type=jnp.float32
    )


def outer_rows(left, right):
    return lax.dot_general(
        left, right, (((0,), (0,)), ((), ())), preferred_element_type=jnp.float32
    )


def smooth_gate(values):
    return jax.nn.gelu(values, approximate=True)


def normalize(values, gain):
    factor = lax.rsqrt(jnp.mean(values * values, axis=1, keepdims=True) + EPSILON)
    unit_rows = values * factor
    return ((unit_rows * gain).astype(jnp.bfloat16), unit_rows, factor)


def normalize_back(values, unit_rows, factor, gain, grad_rows):
    gain_grad = jnp.sum(grad_rows * unit_rows, axis=0)
    scaled = grad_rows * gain
    inner = jnp.mean(scaled * values, axis=1, keepdims=True)
    return (gain_grad, factor * scaled - unit_rows * factor * factor * inner)


def split_heads(values):
    return values.reshape(values.shape[0], -1, HEAD_DIM).transpose(1, 0, 2)


def join_heads(values):
    return values.transpose(1, 0, 2).reshape(values.shape[1], -1)


def read_slots(group_map, reader, holders, rows_each, capacity):
    matched = (group_map.reshape(holders, rows_each) == reader).astype(jnp.int32)
    ranks = jnp.cumsum(matched, axis=1) - 1
    counts = jnp.sum(matched, axis=1)
    place = lax.iota(jnp.int32, holders * capacity)
    valid = place % capacity < jnp.repeat(counts, capacity, total_repeat_length=holders * capacity)
    anchor = lax.iota(jnp.int32, holders)[:, None] * capacity + ranks
    target = jnp.where(matched > 0, anchor, holders * capacity)
    return (valid, target.reshape(-1))


def attend_forward(queries, keys, values, allowed):
    factor = HEAD_DIM ** (-0.5)

    def one_head(parts):
        query, key_rows, value_rows = parts
        scores = jnp.where(allowed, project_back(query, key_rows) * factor, MASKED)
        highest = jnp.max(scores, axis=1, keepdims=True)
        exponent = jnp.exp(scores - highest)
        total = jnp.sum(exponent, axis=1, keepdims=True)
        soft_weights = (exponent / total).astype(jnp.bfloat16)
        return (project(soft_weights, value_rows), (highest + jnp.log(total))[:, 0])

    context, log_total = lax.map(
        one_head, (split_heads(queries), split_heads(keys), split_heads(values))
    )
    return (join_heads(context).astype(jnp.bfloat16), log_total)


def attend_backward(queries, keys, values, context_grad, log_total, allowed):
    factor = HEAD_DIM ** (-0.5)

    def one_head(parts):
        query, key_rows, value_rows, grad_rows, log_row = parts
        scores = jnp.where(allowed, project_back(query, key_rows) * factor, MASKED)
        soft = jnp.exp(scores - log_row[:, None])
        soft_grad = project_back(grad_rows, value_rows)
        score_grad = (soft * (soft_grad - jnp.sum(soft * soft_grad, axis=1, keepdims=True))).astype(
            jnp.bfloat16
        )
        query_grad = project(score_grad, key_rows) * factor
        key_grad = outer_rows(score_grad, query) * factor
        value_grad = outer_rows(soft.astype(jnp.bfloat16), grad_rows)
        return (query_grad, key_grad, value_grad)

    grads = lax.map(
        one_head,
        (
            split_heads(queries),
            split_heads(keys),
            split_heads(values),
            split_heads(context_grad),
            log_total,
        ),
    )
    return (join_heads(grads[0]), join_heads(grads[1]), join_heads(grads[2]))


def heads_total(partial_rows):
    return lax.psum(partial_rows, "tp")


def input_total(partial_rows):
    return lax.psum(partial_rows.astype(jnp.bfloat16), "tp").astype(jnp.float32)


def merge_softmax(first, second):
    highest = jnp.maximum(first[0], second[0])
    total = first[1] * jnp.exp(first[0] - highest) + second[1] * jnp.exp(second[0] - highest)
    return (highest, total, first[2] + second[2])


def body(
    layer_input,
    memory,
    reader_map,
    target_ids,
    target_lengths,
    out_grad,
    self_q,
    self_k,
    self_v,
    self_o,
    cross_q,
    cross_k,
    cross_v,
    cross_o,
    ff_gate,
    ff_up,
    ff_out,
    gain_self,
    gain_cross,
    gain_ff,
    gain_exit,
    exit_table,
):
    (
        w_query,
        w_key,
        w_value,
        w_output,
        c_query,
        c_key,
        c_value,
        c_output,
        w_gate,
        w_up,
        w_down,
        full_gain_self,
        full_gain_cross,
        full_gain_ff,
        full_gain_exit,
    ) = (
        lax.all_gather(self_q, "wide", axis=0, tiled=True),
        lax.all_gather(self_k, "wide", axis=0, tiled=True),
        lax.all_gather(self_v, "wide", axis=0, tiled=True),
        lax.all_gather(self_o, "wide", axis=0, tiled=True),
        lax.all_gather(cross_q, "wide", axis=0, tiled=True),
        lax.all_gather(cross_k, "wide", axis=0, tiled=True),
        lax.all_gather(cross_v, "wide", axis=0, tiled=True),
        lax.all_gather(cross_o, "wide", axis=0, tiled=True),
        lax.all_gather(ff_gate, "wide", axis=0, tiled=True),
        lax.all_gather(ff_up, "wide", axis=0, tiled=True),
        lax.all_gather(ff_out, "wide", axis=0, tiled=True),
        lax.all_gather(gain_self, "wide", axis=0, tiled=True),
        lax.all_gather(gain_cross, "wide", axis=0, tiled=True),
        lax.all_gather(gain_ff, "wide", axis=0, tiled=True),
        lax.all_gather(gain_exit, "wide", axis=0, tiled=True),
    )
    gain_one = full_gain_self.astype(jnp.float32)
    gain_two = full_gain_cross.astype(jnp.float32)
    gain_three = full_gain_ff.astype(jnp.float32)
    gain_last = full_gain_exit.astype(jnp.float32)
    seq_rows = layer_input.shape[0]
    wide_count = lax.axis_size("wide")
    wide_index = lax.axis_index("wide")
    group_index = lax.axis_index("grp")
    group_lengths = lax.dynamic_slice_in_dim(target_lengths, group_index * wide_count, wide_count)
    own_length = lax.dynamic_index_in_dim(group_lengths, wide_index, keepdims=False)
    hidden = layer_input.astype(jnp.float32)
    norm_self, unit_self, factor_self = normalize(hidden, gain_one)
    queries = project(norm_self, w_query).astype(jnp.bfloat16)
    keys = project(norm_self, w_key).astype(jnp.bfloat16)
    values = project(norm_self, w_value).astype(jnp.bfloat16)
    position = lax.iota(jnp.int32, seq_rows)
    allowed_self = (position[None, :] <= position[:, None]) & (position[None, :] < own_length)
    context_self, log_self = attend_forward(queries, keys, values, allowed_self)
    resid_one = hidden + heads_total(project_back(context_self, w_output))
    norm_cross, unit_cross, factor_cross = normalize(resid_one, gain_two)
    cross_queries = project(norm_cross, c_query).astype(jnp.bfloat16)
    memory_keys = project(memory, c_key).astype(jnp.bfloat16)
    memory_values = project(memory, c_value).astype(jnp.bfloat16)
    rows_each = memory.shape[0]
    capacity = max(2, 2 * rows_each // wide_count)
    slot_count = wide_count * capacity
    slot_valid, slot_target = read_slots(reader_map, wide_index, wide_count, rows_each, capacity)
    keys_all, values_all = (
        lax.all_gather(memory_keys, "wide", axis=0, tiled=True),
        lax.all_gather(memory_values, "wide", axis=0, tiled=True),
    )
    read_table = (
        jnp.zeros((slot_count,), jnp.int32)
        .at[slot_target]
        .set(lax.iota(jnp.int32, wide_count * rows_each), mode="drop")
    )
    keys_read = jnp.take(keys_all, read_table, axis=0)
    values_read = jnp.take(values_all, read_table, axis=0)
    allowed_cross = slot_valid[None, :]
    context_cross, log_cross = attend_forward(cross_queries, keys_read, values_read, allowed_cross)
    resid_two = resid_one + heads_total(project_back(context_cross, c_output))
    norm_ff, unit_ff, factor_ff = normalize(resid_two, gain_three)
    gate_float = project(norm_ff, w_gate).astype(jnp.bfloat16).astype(jnp.float32)
    up_float = project(norm_ff, w_up).astype(jnp.bfloat16).astype(jnp.float32)
    gelu_value, gelu_pull = jax.vjp(smooth_gate, gate_float)
    ff_hidden = (gelu_value * up_float).astype(jnp.bfloat16)
    resid_three = resid_two + heads_total(project_back(ff_hidden, w_down))
    block_output = resid_three.astype(jnp.bfloat16)
    norm_exit, unit_exit, factor_exit = normalize(resid_three, gain_last)
    rows_all = lax.all_gather(norm_exit, "wide", axis=0, tiled=True)
    group_tokens = rows_all.shape[0]
    vocab_rows = exit_table.shape[0]
    scale_exit = float(rows_all.shape[1]) ** (-0.5)
    logits = project_back(rows_all, exit_table) * scale_exit
    vocab_ids = lax.axis_index(("wide", "tp")) * vocab_rows + lax.iota(jnp.int32, vocab_rows)
    is_target = target_ids[:, None] == vocab_ids[None, :]
    local_high = jnp.max(logits, axis=1)
    local_total = jnp.sum(jnp.exp(logits - local_high[:, None]), axis=1)
    local_pick = jnp.sum(jnp.where(is_target, logits, 0.0), axis=1)
    highest, total_exp, target_logit = merged(
        (local_high, local_total, local_pick), ("wide", "tp"), merge_softmax
    )
    log_total = highest + jnp.log(total_exp)
    token_place = lax.iota(jnp.int32, group_tokens)
    valid = token_place % seq_rows < jnp.repeat(
        group_lengths, seq_rows, total_repeat_length=group_tokens
    )
    token_count = jnp.sum(target_lengths).astype(jnp.float32)
    token_weight = jnp.where(valid, 1.0, 0.0).astype(jnp.float32) / token_count
    group_loss = jnp.sum(token_weight * (log_total - target_logit))
    logit_grad = (
        (jnp.exp(logits - log_total[:, None]) - jnp.where(is_target, 1.0, 0.0))
        * token_weight[:, None]
    ).astype(jnp.bfloat16)
    rows_grad_all = project(logit_grad, exit_table) * scale_exit
    exit_grad = outer_rows(logit_grad, rows_all) * scale_exit
    rows_part = lax.psum_scatter(
        rows_grad_all.astype(jnp.bfloat16), "wide", scatter_dimension=0, tiled=True
    )
    norm_exit_grad = lax.psum(rows_part, "tp").astype(jnp.float32)
    gain_exit_grad, back_exit = normalize_back(
        resid_three, unit_exit, factor_exit, gain_last, norm_exit_grad
    )
    resid_three_grad = out_grad.astype(jnp.float32) + back_exit
    ff_branch = resid_three_grad.astype(jnp.bfloat16)
    w_down_grad = outer_rows(ff_branch, ff_hidden)
    hidden_grad = project(ff_branch, w_down)
    gate_grad = gelu_pull(hidden_grad * up_float)[0].astype(jnp.bfloat16)
    up_grad = (hidden_grad * gelu_value).astype(jnp.bfloat16)
    w_gate_grad = outer_rows(norm_ff, gate_grad)
    w_up_grad = outer_rows(norm_ff, up_grad)
    norm_ff_grad = input_total(project_back(gate_grad, w_gate) + project_back(up_grad, w_up))
    gain_ff_grad, back_ff = normalize_back(resid_two, unit_ff, factor_ff, gain_three, norm_ff_grad)
    resid_two_grad = resid_three_grad + back_ff
    cross_branch = resid_two_grad.astype(jnp.bfloat16)
    c_output_grad = outer_rows(cross_branch, context_cross)
    cross_context_grad = project(cross_branch, c_output).astype(jnp.bfloat16)
    cross_query_grad, keys_grad_read, values_grad_read = attend_backward(
        cross_queries, keys_read, values_read, cross_context_grad, log_cross, allowed_cross
    )
    empty_grads = jnp.zeros((wide_count * rows_each, keys_grad_read.shape[1]), jnp.float32)
    keys_grad_all = empty_grads.at[read_table].add(keys_grad_read)
    values_grad_all = empty_grads.at[read_table].add(values_grad_read)
    keys_grad, values_grad = (
        lax.psum_scatter(
            keys_grad_all.astype(jnp.bfloat16), "wide", scatter_dimension=0, tiled=True
        ).astype(jnp.float32),
        lax.psum_scatter(
            values_grad_all.astype(jnp.bfloat16), "wide", scatter_dimension=0, tiled=True
        ).astype(jnp.float32),
    )
    keys_grad = keys_grad.astype(jnp.bfloat16)
    values_grad = values_grad.astype(jnp.bfloat16)
    cross_query_grad = cross_query_grad.astype(jnp.bfloat16)
    c_query_grad = outer_rows(norm_cross, cross_query_grad)
    c_key_grad = outer_rows(memory, keys_grad)
    c_value_grad = outer_rows(memory, values_grad)
    norm_cross_grad, memory_grad = (
        lax.psum(project_back(cross_query_grad, c_query).astype(jnp.bfloat16), "tp").astype(
            jnp.float32
        ),
        lax.psum(
            (project_back(keys_grad, c_key) + project_back(values_grad, c_value)).astype(
                jnp.bfloat16
            ),
            "tp",
        ).astype(jnp.float32),
    )
    gain_cross_grad, back_cross = normalize_back(
        resid_one, unit_cross, factor_cross, gain_two, norm_cross_grad
    )
    resid_one_grad = resid_two_grad + back_cross
    self_branch = resid_one_grad.astype(jnp.bfloat16)
    w_output_grad = outer_rows(self_branch, context_self)
    self_context_grad = project(self_branch, w_output).astype(jnp.bfloat16)
    query_grad, key_grad, value_grad = attend_backward(
        queries, keys, values, self_context_grad, log_self, allowed_self
    )
    query_grad = query_grad.astype(jnp.bfloat16)
    key_grad = key_grad.astype(jnp.bfloat16)
    value_grad = value_grad.astype(jnp.bfloat16)
    w_query_grad = outer_rows(norm_self, query_grad)
    w_key_grad = outer_rows(norm_self, key_grad)
    w_value_grad = outer_rows(norm_self, value_grad)
    norm_self_grad = input_total(
        project_back(query_grad, w_query)
        + project_back(key_grad, w_key)
        + project_back(value_grad, w_value)
    )
    gain_self_grad, back_self = normalize_back(
        hidden, unit_self, factor_self, gain_one, norm_self_grad
    )
    input_grad = resid_one_grad + back_self
    shards = (
        lax.psum_scatter(
            w_query_grad.astype(jnp.bfloat16), "wide", scatter_dimension=0, tiled=True
        ).astype(jnp.float32),
        lax.psum_scatter(
            w_key_grad.astype(jnp.bfloat16), "wide", scatter_dimension=0, tiled=True
        ).astype(jnp.float32),
        lax.psum_scatter(
            w_value_grad.astype(jnp.bfloat16), "wide", scatter_dimension=0, tiled=True
        ).astype(jnp.float32),
        lax.psum_scatter(
            w_output_grad.astype(jnp.bfloat16), "wide", scatter_dimension=0, tiled=True
        ).astype(jnp.float32),
        lax.psum_scatter(
            c_query_grad.astype(jnp.bfloat16), "wide", scatter_dimension=0, tiled=True
        ).astype(jnp.float32),
        lax.psum_scatter(
            c_key_grad.astype(jnp.bfloat16), "wide", scatter_dimension=0, tiled=True
        ).astype(jnp.float32),
        lax.psum_scatter(
            c_value_grad.astype(jnp.bfloat16), "wide", scatter_dimension=0, tiled=True
        ).astype(jnp.float32),
        lax.psum_scatter(
            c_output_grad.astype(jnp.bfloat16), "wide", scatter_dimension=0, tiled=True
        ).astype(jnp.float32),
        lax.psum_scatter(
            w_gate_grad.astype(jnp.bfloat16), "wide", scatter_dimension=0, tiled=True
        ).astype(jnp.float32),
        lax.psum_scatter(
            w_up_grad.astype(jnp.bfloat16), "wide", scatter_dimension=0, tiled=True
        ).astype(jnp.float32),
        lax.psum_scatter(
            w_down_grad.astype(jnp.bfloat16), "wide", scatter_dimension=0, tiled=True
        ).astype(jnp.float32),
        lax.psum_scatter(
            gain_self_grad.astype(jnp.bfloat16), "wide", scatter_dimension=0, tiled=True
        ).astype(jnp.float32),
        lax.psum_scatter(
            gain_cross_grad.astype(jnp.bfloat16), "wide", scatter_dimension=0, tiled=True
        ).astype(jnp.float32),
        lax.psum_scatter(
            gain_ff_grad.astype(jnp.bfloat16), "wide", scatter_dimension=0, tiled=True
        ).astype(jnp.float32),
        lax.psum_scatter(
            gain_exit_grad.astype(jnp.bfloat16), "wide", scatter_dimension=0, tiled=True
        ).astype(jnp.float32),
    )
    totals = (
        lax.psum(shards[0].astype(jnp.bfloat16), "grp").astype(jnp.float32),
        lax.psum(shards[1].astype(jnp.bfloat16), "grp").astype(jnp.float32),
        lax.psum(shards[2].astype(jnp.bfloat16), "grp").astype(jnp.float32),
        lax.psum(shards[3].astype(jnp.bfloat16), "grp").astype(jnp.float32),
        lax.psum(shards[4].astype(jnp.bfloat16), "grp").astype(jnp.float32),
        lax.psum(shards[5].astype(jnp.bfloat16), "grp").astype(jnp.float32),
        lax.psum(shards[6].astype(jnp.bfloat16), "grp").astype(jnp.float32),
        lax.psum(shards[7].astype(jnp.bfloat16), "grp").astype(jnp.float32),
        lax.psum(shards[8].astype(jnp.bfloat16), "grp").astype(jnp.float32),
        lax.psum(shards[9].astype(jnp.bfloat16), "grp").astype(jnp.float32),
        lax.psum(shards[10].astype(jnp.bfloat16), "grp").astype(jnp.float32),
        lax.psum(shards[11].astype(jnp.bfloat16), "grp").astype(jnp.float32),
        lax.psum(shards[12].astype(jnp.bfloat16), "grp").astype(jnp.float32),
        lax.psum(shards[13].astype(jnp.bfloat16), "grp").astype(jnp.float32),
        lax.psum(shards[14].astype(jnp.bfloat16), "grp").astype(jnp.float32),
        lax.psum(exit_grad.astype(jnp.bfloat16), "grp").astype(jnp.float32),
        lax.psum(group_loss.astype(jnp.bfloat16), "grp").astype(jnp.float32),
    )
    return (
        block_output,
        totals[16],
        input_grad,
        memory_grad,
        totals[0],
        totals[1],
        totals[2],
        totals[3],
        totals[4],
        totals[5],
        totals[6],
        totals[7],
        totals[8],
        totals[9],
        totals[10],
        totals[11],
        totals[12],
        totals[13],
        totals[14],
        totals[15],
    )


def solution(mesh):
    placed = (
        P(("grp", "wide"), None),
        P(("grp", "wide"), None),
        P("grp"),
        P("grp"),
        P(),
        P(("grp", "wide"), None),
        P("wide", "tp"),
        P("wide", "tp"),
        P("wide", "tp"),
        P("wide", "tp"),
        P("wide", "tp"),
        P("wide", "tp"),
        P("wide", "tp"),
        P("wide", "tp"),
        P("wide", "tp"),
        P("wide", "tp"),
        P("wide", "tp"),
        P("wide"),
        P("wide"),
        P("wide"),
        P("wide"),
        P(("wide", "tp"), None),
    )
    return jax.shard_map(
        body,
        mesh=mesh,
        in_specs=placed,
        out_specs=(
            P(("grp", "wide"), None),
            P(),
            P(("grp", "wide"), None),
            P(("grp", "wide"), None),
            P("wide", "tp"),
            P("wide", "tp"),
            P("wide", "tp"),
            P("wide", "tp"),
            P("wide", "tp"),
            P("wide", "tp"),
            P("wide", "tp"),
            P("wide", "tp"),
            P("wide", "tp"),
            P("wide", "tp"),
            P("wide", "tp"),
            P("wide"),
            P("wide"),
            P("wide"),
            P("wide"),
            P(("wide", "tp"), None),
        ),
        check_vma=False,
    )
```

profile of v0, /device:TPU:19, one launch (start us, length us, event | category | flops | bytes accessed | tf_op | source)
XLA Modules:
  0.0 1302.2 jit_solution(12872729175637967752)
XLA Ops:
  24.9 14.7 %all_gather.67 = bf16[768,384]{1,0:T(8,128)(2,1)S(1)} all-gather(bf16[192,384]{1,0:T(8,128)(2,1)} %param.44), channel_id=1, replica_groups=mesh['grp'=4,'wide'=4,'tp'=2] {'wide'}, dimensions={0}, use_global_device_ids=true | all-gather | bytes 737280 | tf_op jit(solution)/shard_map/all_gather | solution.py:182
  42.3 13.1 %all_gather.68 = bf16[768,384]{1,0:T(8,128)(2,1)S(1)} all-gather(bf16[192,384]{1,0:T(8,128)(2,1)S(1)} %copy-done.49), channel_id=1, replica_groups=mesh['grp'=4,'wide'=4,'tp'=2] {'wide'}, dimensions={0}, use_global_device_ids=true | all-gather | bytes 737280 | tf_op jit(solution)/shard_map/all_gather | solution.py:183
  57.1 12.3 all_gather.69
  71.7 15.2 %while.78 = (s32[]{:T(128)}, bf16[6,256,64]{1,2,0:T(8,128)(2,1)S(1)}, f32[6,256]{1,0:T(8,128)}, bf16[6,256,64]{2,1,0:T(8,128)(2,1)S(1)}, bf16[6,256,64]{2,1,0:T(...) while((s32[]{:T(128)}, ...), condition=%wide.region_4.5_spmd.clone, body=%wide.region_1.4_spmd.clone.sunk | while | flops 17432320 | bytes 1061473 | solution.py:92
  119.7 16.5 %all_gather.74 = bf16[1024,384]{1,0:T(8,128)(2,1)S(1)} all-gather(bf16[256,384]{1,0:T(8,128)(2,1)S(1)} %convolution_convert_fusion.17), channel_id=1, replica_groups=mesh['grp'=4,'wide'=4,'tp'=2] {'wide'}, dimensions={0}, use_global_device_ids=true | all-gather | bytes 983040 | tf_op jit(solution)/shard_map/all_gather | solution.py:226
  136.2 14.1 %all_gather.75 = bf16[768,384]{1,0:T(8,128)(2,1)S(1)} all-gather(bf16[192,384]{1,0:T(8,128)(2,1)S(1)} %copy-done.53), channel_id=1, replica_groups=mesh['grp'=4,'wide'=4,'tp'=2] {'wide'}, dimensions={0}, use_global_device_ids=true | all-gather | bytes 737280 | tf_op jit(solution)/shard_map/all_gather | solution.py:188
  151.2 13.5 %all_gather.76 = bf16[1024,384]{1,0:T(8,128)(2,1)S(1)} all-gather(bf16[256,384]{1,0:T(8,128)(2,1)S(1)} %convolution_convert_fusion.16), channel_id=1, replica_groups=mesh['grp'=4,'wide'=4,'tp'=2] {'wide'}, dimensions={0}, use_global_device_ids=true | all-gather | bytes 983040 | tf_op jit(solution)/shard_map/all_gather | solution.py:227
  171.6 15.4 %all_gather.72 = bf16[768,384]{1,0:T(8,128)(2,1)} all-gather(bf16[192,384]{1,0:T(8,128)(2,1)S(1)} %copy-done.54), channel_id=1, replica_groups=mesh['grp'=4,'wide'=4,'tp'=2] {'wide'}, dimensions={0}, use_global_device_ids=true | all-gather | bytes 737280 | tf_op jit(solution)/shard_map/all_gather | solution.py:186
  203.6 35.0 %while.79 = (s32[]{:T(128)}, bf16[6,256,64]{1,2,0:T(8,128)(2,1)}, f32[6,256]{1,0:T(8,128)S(1)}, bf16[6,256,64]{2,1,0:T(8,128)(2,1)}, bf16[6,512,64]{2,1,0:T(8,12...) while((s32[]{:T(128)}, bf16[6,256,64]{1,2,0:T(8,128)(2,1)}, ...), condition=%wide.region_14.16_spmd.clone, body=%wide.region_11.15_spmd.clone.sunk | while | flops 34615552 | bytes 1991817 | solution.py:92
  243.3 61.9 %all-reduce.24.cloned.1.call-done = f32[256,768]{1,0:T(8,128)} async-done(((f32[256,768]{1,0:T(8,128)}), f32[256,768]{1,0:T(8,128)}) %all-reduce.24.cloned.1.call-update) | async-done | bytes 786448 | tf_op jit(solution)/shard_map/psum | solution.py:128
  312.1 34.5 %all-gather.8.cloned.1.call-done = bf16[768,1024]{1,0:T(8,128)(2,1)} async-done(((bf16[192,1024]{1,0:T(8,128)(2,1)}), bf16[768,1024]{1,0:T(8,128)(2,1)}) %all-gather.8.cloned.1.call-update) | async-done | bytes 1572880 | tf_op jit(solution)/shard_map/all_gather | solution.py:190
  348.6 35.2 %all-gather.12.cloned.1.call-done = bf16[768,1024]{1,0:T(8,128)(2,1)} async-done(((bf16[192,1024]{1,0:T(8,128)(2,1)}), bf16[768,1024]{1,0:T(8,128)(2,1)}) %all-gather.12.cloned.1.call-update) | async-done | bytes 1572880 | tf_op jit(solution)/shard_map/all_gather | solution.py:192
  387.4 33.6 %all-reduce.26.cloned.1.call-done = f32[256,768]{1,0:T(8,128)} async-done(((f32[256,768]{1,0:T(8,128)}), f32[256,768]{1,0:T(8,128)}) %all-reduce.26.cloned.1.call-update) | async-done | bytes 786448 | tf_op jit(solution)/shard_map/psum | solution.py:128
  427.2 32.7 %all-gather.14.cloned.1.call-done = bf16[1024,768]{1,0:T(8,128)(2,1)} async-done(((bf16[256,768]{1,0:T(8,128)(2,1)}), bf16[1024,768]{1,0:T(8,128)(2,1)}) %all-gather.14.cloned.1.call-update) | async-done | bytes 1572880 | tf_op jit(solution)/shard_map/all_gather | solution.py:247
  475.0 19.0 %all-gather.2 = bf16[8192]{0:T(1024)(128)(2,1)} all-gather(bf16[1024]{0:T(1024)(128)(2,1)S(1)} %get-tuple-element.718), channel_id=4, replica_groups=mesh['grp'=4,'wide'=4,'tp'=2] {'wide','tp'}, dimensions={0}, use_global_device_ids=true | all-gather | bytes 18432 | tf_op jit(solution)/shard_map/all_gather | solution.py:15
  496.0 21.4 %all-gather.1 = bf16[8192]{0:T(1024)(128)(2,1)} all-gather(bf16[1024]{0:T(1024)(128)(2,1)S(1)} %get-tuple-element.719), channel_id=3, replica_groups=mesh['grp'=4,'wide'=4,'tp'=2] {'wide','tp'}, dimensions={0}, use_global_device_ids=true | all-gather | bytes 18432 | tf_op jit(solution)/shard_map/all_gather | solution.py:15
  519.4 21.4 %all-gather = bf16[8192]{0:T(1024)(128)(2,1)} all-gather(bf16[1024]{0:T(1024)(128)(2,1)S(1)} %convert_element_type.487), channel_id=2, replica_groups=mesh['grp'=4,'wide'=4,'tp'=2] {'wide','tp'}, dimensions={0}, use_global_device_ids=true | all-gather | bytes 18432 | tf_op jit(solution)/shard_map/all_gather | solution.py:15
  580.1 51.7 %reduce-scatter.19.cloned.1.call-done = bf16[256,768]{1,0:T(8,128)(2,1)} async-done(((bf16[1024,768]{1,0:T(8,128)(2,1)}), bf16[256,768]{1,0:T(8,128)(2,1)}) %reduce-scatter.19.cloned.1.call-update) | async-done | bytes 393232 | tf_op jit(solution)/shard_map/reduce_scatter | solution.py:274
  632.0 24.8 %all-reduce.28.cloned.1.call-done = bf16[256,768]{1,0:T(8,128)(2,1)} async-done(((bf16[256,768]{1,0:T(8,128)(2,1)}), bf16[256,768]{1,0:T(8,128)(2,1)}) %all-reduce.28.cloned.1.call-update) | async-done | bytes 393232 | tf_op jit(solution)/shard_map/psum | solution.py:277
  665.1 25.8 %all-reduce.30.cloned.1.call-done = bf16[256,768]{1,0:T(8,128)(2,1)} async-done(((bf16[256,768]{1,0:T(8,128)(2,1)}), bf16[256,768]{1,0:T(8,128)(2,1)}) %all-reduce.30.cloned.1.call-update) | async-done | bytes 393232 | tf_op jit(solution)/shard_map/psum | solution.py:132
  697.2 65.4 %while.80 = (s32[]{:T(128)}, bf16[6,256,64]{1,2,0:T(8,128)(2,1)}, f32[6,512,64]{1,2,0:T(8,128)}, f32[6,512,64]{1,2,0:T(8,128)}, bf16[6,256,64]{2,1,0:T(8,128)(2,...) while((s32[]{:T(128)}, bf16[6,256,64]{1,2,0:T(8,128)(2,1)}, ...), condition=%wide.region_34.36_spmd.clone, body=%wide.region_32.35_spmd.clone.sunk | while | flops 85127424 | bytes 4873369 | solution.py:114
  796.4 22.9 %reduce-scatter.23.cloned.1.call-done = bf16[256,384]{1,0:T(8,128)(2,1)} async-done(((bf16[1024,384]{1,0:T(8,128)(2,1)}), bf16[256,384]{1,0:T(8,128)(2,1)}) %reduce-scatter.23.cloned.1.call-update) | async-done | bytes 196624 | tf_op jit(solution)/shard_map/reduce_scatter | solution.py:305
  832.4 31.0 %while.81 = (s32[]{:T(128)}, bf16[6,256,64]{1,2,0:T(8,128)(2,1)S(1)}, bf16[6,256,64]{1,2,0:T(8,128)(2,1)S(1)}, bf16[6,256,64]{1,2,0:T(8,128)(2,1)S(1)}, bf16[6,2...) while((s32[]{:T(128)}, ...), condition=%wide.region_39.41_spmd.clone, body=%wide.region_37.40_spmd.clone.sunk | while | flops 42696448 | bytes 2566769 | solution.py:114
  896.0 14.8 %reduce-scatter.35.cloned.1.call-done = bf16[192,384]{1,0:T(8,128)(2,1)} async-done(((bf16[768,384]{1,0:T(8,128)(2,1)}), bf16[192,384]{1,0:T(8,128)(2,1)}) %reduce-scatter.35.cloned.1.call-update) | async-done | bytes 147472 | tf_op jit(solution)/shard_map/reduce_scatter | solution.py:373
  910.8 22.7 %reduce-scatter.31.cloned.1.call-done = bf16[192,384]{1,0:T(8,128)(2,1)} async-done(((bf16[768,384]{1,0:T(8,128)(2,1)}), bf16[192,384]{1,0:T(8,128)(2,1)}) %reduce-scatter.31.cloned.1.call-update) | async-done | bytes 147472 | tf_op jit(solution)/shard_map/reduce_scatter | solution.py:361
  933.5 23.2 %reduce-scatter.25.cloned.1.call-done = bf16[192,384]{1,0:T(8,128)(2,1)} async-done(((bf16[768,384]{1,0:T(8,128)(2,1)}), bf16[192,384]{1,0:T(8,128)(2,1)}) %reduce-scatter.25.cloned.1.call-update) | async-done | bytes 147472 | tf_op jit(solution)/shard_map/reduce_scatter | solution.py:352
  956.8 23.4 %reduce-scatter.27.cloned.1.call-done = bf16[192,384]{1,0:T(8,128)(2,1)} async-done(((bf16[768,384]{1,0:T(8,128)(2,1)}), bf16[192,384]{1,0:T(8,128)(2,1)}) %reduce-scatter.27.cloned.1.call-update) | async-done | bytes 147472 | tf_op jit(solution)/shard_map/reduce_scatter | solution.py:355
  980.1 22.8 %reduce-scatter.29.cloned.1.call-done = bf16[192,384]{1,0:T(8,128)(2,1)} async-done(((bf16[768,384]{1,0:T(8,128)(2,1)}), bf16[192,384]{1,0:T(8,128)(2,1)}) %reduce-scatter.29.cloned.1.call-update) | async-done | bytes 147472 | tf_op jit(solution)/shard_map/reduce_scatter | solution.py:358
  1002.9 38.5 %reduce-scatter.41.cloned.1.call-done = bf16[192,1024]{1,0:T(8,128)(2,1)} async-done(((bf16[768,1024]{1,0:T(8,128)(2,1)}), bf16[192,1024]{1,0:T(8,128)(2,1)}) %reduce-scatter.41.cloned.1.call-update) | async-done | bytes 393232 | tf_op jit(solution)/shard_map/reduce_scatter | solution.py:382
  1041.5 36.6 %reduce-scatter.39.cloned.1.call-done = bf16[192,1024]{1,0:T(8,128)(2,1)} async-done(((bf16[768,1024]{1,0:T(8,128)(2,1)}), bf16[192,1024]{1,0:T(8,128)(2,1)}) %reduce-scatter.39.cloned.1.call-update) | async-done | bytes 393232 | tf_op jit(solution)/shard_map/reduce_scatter | solution.py:379
  1078.1 36.6 %reduce-scatter.37.cloned.1.call-done = bf16[192,1024]{1,0:T(8,128)(2,1)} async-done(((bf16[768,1024]{1,0:T(8,128)(2,1)}), bf16[192,1024]{1,0:T(8,128)(2,1)}) %reduce-scatter.37.cloned.1.call-update) | async-done | bytes 393232 | tf_op jit(solution)/shard_map/reduce_scatter | solution.py:376
  1138.7 136.9 %all-reduce.34.cloned.1.call-done = (bf16[192,384]{0,1:T(8,128)(2,1)}, bf16[192,384]{0,1:T(8,128)(2,1)}, bf16[192,384]{1,0:T(8,128)(2,1)}, bf16[192,384]{1,0:T(8...) async-done(((bf16[192,384]{0,1:T(8,128)(2,1)}, ...) | async-done | bytes 8527888 | tf_op jit(solution)/shard_map/psum | solution.py:404
  (602 shorter events, 450.6 us)
Async XLA Ops:
  8.0 111.3 %copy-start = (bf16[256,768]{1,0:T(8,128)(2,1)S(1)}, bf16[256,768]{1,0:T(8,128)(2,1)}, u32[]{:S(2)}) copy-start(bf16[256,768]{1,0:T(8,128)(2,1)} %param.39) | copy-start | bytes 1179652
  8.1 190.7 %all-reduce.22.cloned.1.call-start = ((), (), s32[]{:S(2)}) async-start(), calls=%async_computation.14 | async-start | bytes 1572864 | tf_op jit(solution)/shard_map/psum | solution.py:128
  101.1 204.1 %all-reduce.24.cloned.1.call-start = ((), (), s32[]{:S(2)}) async-start(), calls=%async_computation.15 | async-start | bytes 1572864 | tf_op jit(solution)/shard_map/psum | solution.py:128
  107.2 93.1 %copy-start.57 = (f32[768]{0:T(1024)}, f32[768]{0:T(1024)S(1)}, u32[]{:S(2)}) copy-start(f32[768]{0:T(1024)S(1)} %convert_element_type.465) | copy-start | bytes 9220
  241.0 68.4 %all-gather.10.cloned.1.call-start = ((), (), s32[]{:S(2)}) async-start(), calls=%async_computation.17 | async-start | bytes 1966080 | tf_op jit(solution)/shard_map/all_gather | solution.py:191
  241.6 105.1 %all-gather.8.cloned.1.call-start = ((), (), s32[]{:S(2)}) async-start(), calls=%async_computation.16 | async-start | bytes 1966080 | tf_op jit(solution)/shard_map/all_gather | solution.py:190
  242.2 141.7 %all-gather.12.cloned.1.call-start = ((), (), s32[]{:S(2)}) async-start(), calls=%async_computation.18 | async-start | bytes 1966080 | tf_op jit(solution)/shard_map/all_gather | solution.py:192
  242.7 178.2 %all-reduce.26.cloned.1.call-start = ((), (), s32[]{:S(2)}) async-start(), calls=%async_computation.19 | async-start | bytes 1572864 | tf_op jit(solution)/shard_map/psum | solution.py:128
  243.3 105.3 %copy-start.59 = (f32[768]{0:T(1024)}, f32[768]{0:T(1024)S(1)}, u32[]{:S(2)}) copy-start(f32[768]{0:T(1024)S(1)} %convert_element_type.476) | copy-start | bytes 9220
  387.3 72.6 %all-gather.14.cloned.1.call-start = ((), (), s32[]{:S(2)}) async-start(), calls=%async_computation.20 | async-start | bytes 1966080 | tf_op jit(solution)/shard_map/all_gather | solution.py:247
  387.3 82.0 %copy-start.61 = (f32[768]{0:T(1024)}, f32[768]{0:T(1024)S(1)}, u32[]{:S(2)}) copy-start(f32[768]{0:T(1024)S(1)} %convert_element_type.485) | copy-start | bytes 9220
  423.1 208.6 %reduce-scatter.19.cloned.1.call-start = ((), (), s32[]{:S(2)}) async-start(), calls=%async_computation.21 | async-start | bytes 1966080 | tf_op jit(solution)/shard_map/reduce_scatter | solution.py:274
  569.1 87.7 %copy-start.62 = (f32[768]{0:T(1024)S(1)}, f32[768]{0:T(1024)}, u32[]{:S(2)}) copy-start(f32[768]{0:T(1024)} %copy-done.61) | copy-start | bytes 9220
  569.1 87.7 %copy-start.72 = (f32[256]{0:T(256)S(1)}, f32[256]{0:T(256)}, u32[]{:S(2)}) copy-start(f32[256]{0:T(256)} %copy-done.71) | copy-start | bytes 3076
  580.0 76.7 %all-reduce.28.cloned.1.call-start = ((), (), s32[]{:S(2)}) async-start(), calls=%async_computation.22 | async-start | bytes 786432 | tf_op jit(solution)/shard_map/psum | solution.py:277
  631.8 59.1 %all-reduce.30.cloned.1.call-start = ((), (), s32[]{:S(2)}) async-start(), calls=%async_computation.23 | async-start | bytes 786432 | tf_op jit(solution)/shard_map/psum | solution.py:132
  665.0 129.0 %reduce-scatter.21.cloned.1.call-start = ((), (), s32[]{:S(2)}) async-start(), calls=%async_computation.25 | async-start | bytes 983040 | tf_op jit(solution)/shard_map/reduce_scatter | solution.py:302
  771.3 47.9 %reduce-scatter.23.cloned.1.call-start = ((), (), s32[]{:S(2)}) async-start(), calls=%async_computation.26 | async-start | bytes 983040 | tf_op jit(solution)/shard_map/reduce_scatter | solution.py:305
  781.5 43.8 %all-reduce.32.cloned.1.call-start = ((), (), s32[]{:S(2)}) async-start(), calls=%async_computation.24 | async-start | bytes 786432 | tf_op jit(solution)/shard_map/psum | solution.py:316
  783.9 108.7 %reduce-scatter.43.cloned.1.call-start = ((), (), s32[]{:S(2)}) async-start(), calls=%async_computation.36 | async-start | bytes 737280
  796.3 98.0 %reduce-scatter.45.cloned.1.call-start = ((), (), s32[]{:S(2)}) async-start(), calls=%async_computation.37 | async-start | bytes 737280
  821.6 74.4 %reduce-scatter.33.cloned.1.call-start = ((), (), s32[]{:S(2)}) async-start(), calls=%async_computation.31 | async-start | bytes 737280 | tf_op jit(solution)/shard_map/reduce_scatter | solution.py:364
  824.0 86.9 %reduce-scatter.35.cloned.1.call-start = ((), (), s32[]{:S(2)}) async-start(), calls=%async_computation.32 | async-start | bytes 737280 | tf_op jit(solution)/shard_map/reduce_scatter | solution.py:373
  825.3 108.3 %reduce-scatter.31.cloned.1.call-start = ((), (), s32[]{:S(2)}) async-start(), calls=%async_computation.30 | async-start | bytes 737280 | tf_op jit(solution)/shard_map/reduce_scatter | solution.py:361
  832.3 124.5 %reduce-scatter.25.cloned.1.call-start = ((), (), s32[]{:S(2)}) async-start(), calls=%async_computation.27 | async-start | bytes 737280 | tf_op jit(solution)/shard_map/reduce_scatter | solution.py:352
  864.8 115.4 %reduce-scatter.27.cloned.1.call-start = ((), (), s32[]{:S(2)}) async-start(), calls=%async_computation.28 | async-start | bytes 737280 | tf_op jit(solution)/shard_map/reduce_scatter | solution.py:355
  866.2 136.8 %reduce-scatter.29.cloned.1.call-start = ((), (), s32[]{:S(2)}) async-start(), calls=%async_computation.29 | async-start | bytes 737280 | tf_op jit(solution)/shard_map/reduce_scatter | solution.py:358
  867.5 173.9 %reduce-scatter.41.cloned.1.call-start = ((), (), s32[]{:S(2)}) async-start(), calls=%async_computation.35 | async-start | bytes 1966080 | tf_op jit(solution)/shard_map/reduce_scatter | solution.py:382
  870.8 207.3 %reduce-scatter.39.cloned.1.call-start = ((), (), s32[]{:S(2)}) async-start(), calls=%async_computation.34 | async-start | bytes 1966080 | tf_op jit(solution)/shard_map/reduce_scatter | solution.py:379
  874.3 240.4 %reduce-scatter.37.cloned.1.call-start = ((), (), s32[]{:S(2)}) async-start(), calls=%async_computation.33 | async-start | bytes 1966080 | tf_op jit(solution)/shard_map/reduce_scatter | solution.py:376
  876.2 239.3 %all-reduce.36.cloned.1.call-start = ((), (), s32[]{:S(2)}) async-start(), calls=%async_computation.39 | async-start | bytes 1572864 | tf_op jit(solution)/shard_map/psum | solution.py:132
  881.1 394.5 %all-reduce.34.cloned.1.call-start = ((), (), s32[]{:S(2)}) async-start(), calls=%async_computation.38 | async-start | bytes 17252352 | tf_op jit(solution)/shard_map/psum | solution.py:404
  (75 other events, 1281.8 us)
Sparse Core Ops, SparseCore 0:
  101.2 47.6 all-reduce.21
  241.1 64.0 all-reduce.23
  387.4 33.4 all-reduce.25
  631.9 24.8 all-reduce.27
  665.1 25.7 all-reduce.29
  785.0 26.8 all-reduce.31
  881.2 35.0 all-reduce.35
  1114.9 160.6 all-reduce.33
Sparse Core Ops, SparseCore 1:
  243.0 66.3 all-gather.9
  310.8 35.8 all-gather.7
  348.1 35.8 all-gather.11
  423.2 36.6 all-gather.13
  580.1 51.6 reduce-scatter.18
  771.4 22.5 reduce-scatter.20
  796.7 22.5 reduce-scatter.22
  822.1 19.9 reduce-scatter.42
  844.9 20.5 reduce-scatter.44
  867.8 20.2 reduce-scatter.32
  890.3 20.4 reduce-scatter.34
  913.2 20.2 reduce-scatter.30
  936.4 20.3 reduce-scatter.24
  959.7 20.3 reduce-scatter.26
  982.5 20.3 reduce-scatter.28
  1005.4 36.0 reduce-scatter.40
  1043.9 34.1 reduce-scatter.38
  1080.5 34.1 reduce-scatter.36
where the time goes:
time: 1320 us; the launch traced here: 1300 us
  waiting for transfers between devices  693 us (52%)
  blocking collectives  219 us (17%)
  matrix products  177 us (13%)
  other arithmetic  124 us (9%)
  local copies, waits for them, and re-layouts  64 us (5%)
  between operations  21.4 us (2%)
    psum x1, waiting for transfers between devices, body(): lax.psum(shards[5].astype(jnp.bfloat16), 'grp').astype(jnp.float32)  137 us
    psum x3, waiting for transfers between devices, heads_total(): return lax.psum(partial_rows, 'tp')  95.5 us
    dot_general x48, matrix products, project_back(): lax.dot_general(left, right, (((1,), (1,)), ((), ())), preferred_element_...  65.6 us
    all_gather x3, blocking collectives, merged(): lax.all_gather(part.astype(kind), axis)  61.7 us
    dot_general x36, matrix products, outer_rows(): lax.dot_general(left, right, (((0,), (0,)), ((), ())), preferred_element_...  58.6 us
    dot_general x36, matrix products, project(): return jnp.dot(left, right, preferred_element_type=jnp.float32)  53 us
    reduce_scatter x1, waiting for transfers between devices, body(): lax.psum_scatter(rows_grad_all.astype(jnp.bfloat16), 'wide', scatter_dime...  51.7 us
    reduce_scatter x1, waiting for transfers between devices, body(): lax.psum_scatter(w_down_grad.astype(jnp.bfloat16), 'wide', scatter_dimens...  38.5 us
  transfers between devices with their start and end apart: 26, of which 20 were waited for; matrix products, arithmetic and copies ran while one was open for 9% of the time, Pallas kernels for 0%

commit v1 on v0

--- a/solution.py
+++ b/solution.py
@@ -1,6 +1,8 @@
 import jax
 import jax.numpy as jnp
 from jax import lax
+from jax.experimental import pallas as pl
+from jax.experimental.pallas import tpu as pltpu
 from jax.sharding import PartitionSpec as P
 
 HEAD_DIM = 64
@@ -138,7 +140,7 @@
     return (highest, total, first[2] + second[2])
 
 
-def body(
+def plain_body(
     layer_input,
     memory,
     reader_map,
@@ -438,6 +440,667 @@
     )
 
 
+MESH = pl.DeviceIdType.MESH
+BF = jnp.bfloat16
+F32 = jnp.float32
+
+
+def dot_nn(left, right):
+    return lax.dot_general(left, right, (((1,), (0,)), ((), ())), preferred_element_type=F32)
+
+
+def dot_nt(left, right):
+    return lax.dot_general(left, right, (((1,), (1,)), ((), ())), preferred_element_type=F32)
+
+
+def dot_tn(left, right):
+    return lax.dot_general(left, right, (((0,), (0,)), ((), ())), preferred_element_type=F32)
+
+
+class Move:
+    def __init__(self, out, arrival):
+        self.out, self.arrival = out, arrival
+
+    def start(self):
+        self.out.start()
+        return self
+
+    def sent(self):
+        self.out.wait_send()
+
+    def landed(self):
+        self.arrival.wait_recv()
+
+
+class Links:
+    def __init__(self, send_sems, recv_sems):
+        self.send_sems, self.recv_sems = send_sems, recv_sems
+        self.used = 0
+        self.moves = []
+
+    def move(self, src, dst, device, lands):
+        k = self.used
+        self.used += 1
+        out = pltpu.make_async_remote_copy(
+            src_ref=src, dst_ref=dst, send_sem=self.send_sems.at[k], recv_sem=self.recv_sems.at[k],
+            device_id=device, device_id_type=MESH,
+        )
+        arrival = pltpu.make_async_remote_copy(
+            src_ref=lands, dst_ref=lands, send_sem=self.send_sems.at[k], recv_sem=self.recv_sems.at[k],
+            device_id=device, device_id_type=MESH,
+        )
+        made = Move(out, arrival)
+        self.moves.append(made)
+        return made
+
+    def finish(self):
+        for made in self.moves:
+            made.sent()
+
+
+class Copies:
+    def __init__(self, sems):
+        self.sems, self.used, self.pending = sems, 0, []
+
+    def start(self, src, dst):
+        made = pltpu.make_async_copy(src, dst, self.sems.at[self.used])
+        self.used += 1
+        made.start()
+        return made
+
+    def save(self, src, dst):
+        self.pending.append(self.start(src, dst))
+
+    def finish(self):
+        for made in self.pending:
+            made.wait()
+
+
+def greet(devices):
+    barrier = pltpu.get_barrier_semaphore()
+    for device in devices:
+        pl.semaphore_signal(barrier, inc=1, device_id=device, device_id_type=MESH)
+    pl.semaphore_wait(barrier, len(devices))
+
+
+def rms_rows(values, gain):
+    factor = lax.rsqrt(jnp.mean(values * values, axis=1, keepdims=True) + EPSILON)
+    return (values * factor * gain).astype(BF)
+
+
+def lane_masks():
+    lane = lax.broadcasted_iota(jnp.int32, (1, 2 * HEAD_DIM), 1)
+    low = jnp.where(lane < HEAD_DIM, 1.0, 0.0).astype(F32)
+    return low.astype(BF), (1.0 - low).astype(BF)
+
+
+def both_heads(pair):
+    low, high = lane_masks()
+    return jnp.concatenate([pair * low, pair * high], axis=0)
+
+
+def pick_heads(stacked):
+    rows = stacked.shape[0] // 2
+    lane = lax.broadcasted_iota(jnp.int32, (rows, 2 * HEAD_DIM), 1)
+    return jnp.where(lane < HEAD_DIM, stacked[:rows], stacked[rows:])
+
+
+def pair_columns(p):
+    return pl.ds(pl.multiple_of(p * 2 * HEAD_DIM, 2 * HEAD_DIM), 2 * HEAD_DIM)
+
+
+def attention_forward(pairs, queries, keys, values, probs, context, allowed):
+    factor = HEAD_DIM ** (-0.5)
+
+    def step(p, carry):
+        cols = pair_columns(p)
+        scores = dot_nt(both_heads(queries[:, cols]), keys[:, cols]) * factor
+        scores = jnp.where(allowed, scores, MASKED)
+        exponent = jnp.exp(scores - jnp.max(scores, axis=1, keepdims=True))
+        soft = (exponent / jnp.sum(exponent, axis=1, keepdims=True)).astype(BF)
+        probs[p] = soft
+        context[:, cols] = pick_heads(dot_nn(soft, values[:, cols])).astype(BF)
+        return carry
+
+    lax.fori_loop(0, pairs, step, 0)
+
+
+def forward_kernel(
+    x_ref, mem_ref, map_ref, len_ref, gain_ref,
+    q_in, k_in, v_in, so_in, cq_in, ck_in, cv_in, co_in, ga_in, up_in, dn_in,
+    block_o, one_o, two_o, three_o, exit_o, q_o, k_o, v_o, cq_o, mk_o, mv_o, sc_o, cc_o, ps_o, pc_o,
+    ga_o, up_o, sel_o, wa_o, wgu_o, wd_o, gain_o,
+    wa, wgu, wd, gains, slots, packed, part_out, part_in,
+    block, one, two, three, exit_rows, q, k, v, cq, mk, mv, sc, cc, ps, pc, ga, up, gain_sum,
+    send_sems, recv_sems, copy_sems,
+):
+    count = map_ref.shape[0]
+    g, w, t = lax.axis_index("grp"), lax.axis_index("wide"), lax.axis_index("tp")
+    c = lax.rem(g, 2)
+    left, right, far = (lax.rem(w + d, count) for d in (count - 1, 1, 2))
+    to_left, to_right, to_far = {"wide": left}, {"wide": right}, {"wide": far}
+    to_core, to_tp = {"grp": g + 1 - 2 * c}, {"tp": 1 - t}
+    rows = x_ref.shape[0]
+    links, copies = Links(send_sems, recv_sems), Copies(copy_sems)
+    depth = q_in.shape[0]
+    half = depth // 2
+    wide_cols = dn_in.shape[1] // 2
+
+    def own(at):
+        return pl.ds(pl.multiple_of(at * depth, 16), depth)
+
+    def part(at, which):
+        return pl.ds(pl.multiple_of(at * depth + which * half, 16), half)
+
+    order = (q_in, k_in, v_in, so_in, ck_in, cv_in, cq_in, co_in)
+    placed = []
+    for j in range(4):
+        placed.append([copies.start(order[2 * j + e], wa.at[2 * j + e, own(w)]) for e in range(2)])
+    placed.append([copies.start(ref, wgu.at[e, own(w)]) for e, ref in enumerate((ga_in, up_in))])
+    placed.append(
+        [copies.start(dn_in.at[:, pl.ds(e * wide_cols, wide_cols)], wd.at[e, own(w)]) for e in range(2)]
+    )
+    bufs = [(wa, 2 * j + c, 2 * j + 1 - c) for j in range(4)] + [(wgu, c, 1 - c), (wd, c, 1 - c)]
+    greet([to_left, to_right, to_far, to_core, to_tp])
+
+    gains[w] = gain_ref[...]
+    gain_moves = [
+        links.move(gain_ref, gains.at[w], device, gains.at[at]).start()
+        for device, at in ((to_left, right), (to_right, left), (to_far, far))
+    ]
+
+    item = [{} for _ in bufs]
+
+    def issue(i):
+        buf, mine, other = bufs[i]
+        for made in placed[i]:
+            made.wait()
+        src = buf.at[mine, own(w)]
+        item[i]["from_left"] = links.move(src, src, to_right, buf.at[mine, own(left)]).start()
+        item[i]["from_right"] = links.move(src, src, to_left, buf.at[mine, own(right)]).start()
+
+    def to_other(i, where):
+        buf, mine, other = bufs[i]
+        src = buf.at[mine, where]
+        item[i].setdefault("core", []).append(links.move(src, src, to_core, buf.at[other, where]).start())
+
+    def forward(i):
+        buf, mine, other = bufs[i]
+        item[i]["from_left"].landed()
+        src = buf.at[mine, part(left, 0)]
+        item[i]["far_top"] = links.move(src, src, to_right, buf.at[mine, part(far, 0)]).start()
+        to_other(i, own(left))
+        item[i]["from_right"].landed()
+        src = buf.at[mine, part(right, 1)]
+        item[i]["far_low"] = links.move(src, src, to_left, buf.at[mine, part(far, 1)]).start()
+        to_other(i, own(right))
+
+    def complete(i):
+        item[i]["far_top"].landed()
+        to_other(i, part(far, 0))
+        item[i]["far_low"].landed()
+        to_other(i, part(far, 1))
+
+    def ready(i):
+        for made in item[i]["core"]:
+            made.landed()
+
+    issue(0)
+    issue(1)
+
+    capacity = slots.shape[0] // count
+    readers = map_ref[...]
+    own_map = map_ref[pl.ds(w, 1)]
+    reader_iota = lax.broadcasted_iota(jnp.int32, (max(8, count), rows), 0)
+    matched = jnp.where(reader_iota == own_map, 1.0, 0.0).astype(F32)
+    before = lax.broadcasted_iota(jnp.int32, (rows, rows), 0) < lax.broadcasted_iota(
+        jnp.int32, (rows, rows), 1
+    )
+    ranks = dot_nn(matched.astype(BF), jnp.where(before, 1.0, 0.0).astype(BF))
+    rank = jnp.sum(matched * ranks, axis=0, keepdims=True).astype(jnp.int32)
+    slot_of = own_map * capacity + rank
+    slot_iota = lax.broadcasted_iota(jnp.int32, (slots.shape[0], rows), 0)
+    choose = jnp.where(slot_iota == slot_of, 1.0, 0.0).astype(BF)
+    packed[...] = dot_nn(choose, mem_ref[...]).astype(BF)
+
+    def slot_rows(at, which):
+        return pl.ds(pl.multiple_of(at * capacity + which * (capacity // 2), 16), capacity // 2)
+
+    slot_moves = [
+        links.move(packed.at[slot_rows(to, t)], slots.at[slot_rows(w, t)], device, slots.at[slot_rows(at, t)]).start()
+        for device, to, at in ((to_left, left, right), (to_right, right, left), (to_far, far, far))
+    ]
+    slots[pl.ds(pl.multiple_of(w * capacity, 16), capacity), :] = packed[
+        pl.ds(pl.multiple_of(w * capacity, 16), capacity), :
+    ]
+    issue(2)
+
+    for made in gain_moves:
+        made.landed()
+    total_gain = gains[0]
+    for at in range(1, count):
+        total_gain = total_gain + gains[at]
+    gain_sum[...] = total_gain
+
+    hidden = x_ref[...].astype(F32)
+    norm_self = rms_rows(hidden, gain_sum[0:1, :])
+    forward(0)
+    forward(1)
+    issue(3)
+    complete(0)
+    complete(1)
+    slot_fills = []
+    for made, at in zip(slot_moves, (right, left, far)):
+        made.landed()
+        src = slots.at[slot_rows(at, t)]
+        slot_fills.append(links.move(src, src, to_tp, slots.at[slot_rows(at, 1 - t)]).start())
+    ready(0)
+    q[...] = dot_nn(norm_self, wa[0]).astype(BF)
+    k[...] = dot_nn(norm_self, wa[1]).astype(BF)
+    ready(1)
+    v[...] = dot_nn(norm_self, wa[2]).astype(BF)
+    forward(2)
+    issue(4)
+    length = len_ref[g * count + w]
+    query_at = lax.broadcasted_iota(jnp.int32, (2 * rows, rows), 0)
+    query_at = jnp.where(query_at >= rows, query_at - rows, query_at)
+    key_at = lax.broadcasted_iota(jnp.int32, (2 * rows, rows), 1)
+    allowed_self = (key_at <= query_at) & (key_at < length)
+    pairs = q.shape[1] // (2 * HEAD_DIM)
+    attention_forward(pairs, q, k, v, ps, sc, allowed_self)
+
+    def exchange_start(n):
+        return links.move(part_out.at[n], part_in.at[n], to_tp, part_in.at[n]).start()
+
+    def exchanged(n, made):
+        made.landed()
+        return part_out[n].astype(F32) + part_in[n].astype(F32)
+
+    part_out[0] = dot_nt(sc[...], wa[3]).astype(BF)
+    swap = exchange_start(0)
+    complete(2)
+    forward(3)
+    issue(5)
+    for made in slot_fills:
+        made.landed()
+    ready(2)
+    mk[...] = dot_nn(slots[...], wa[4]).astype(BF)
+    mv[...] = dot_nn(slots[...], wa[5]).astype(BF)
+    complete(3)
+    counts = jnp.sum(jnp.where(readers == w, 1.0, 0.0), axis=1, keepdims=True)
+    slot_lane = lax.broadcasted_iota(jnp.int32, (count, slots.shape[0]), 1)
+    slot_holder = lax.broadcasted_iota(jnp.int32, (count, slots.shape[0]), 0)
+    slot_place = slot_lane - slot_holder * capacity
+    filled = (slot_place >= 0) & (slot_place < capacity) & (slot_place.astype(F32) < counts)
+    valid_slot = jnp.sum(jnp.where(filled, 1.0, 0.0), axis=0, keepdims=True)
+    allowed_cross = jnp.broadcast_to(valid_slot, (2 * rows, slots.shape[0])) > 0.5
+    one[...] = hidden + exchanged(0, swap)
+    norm_cross = rms_rows(one[...], gain_sum[1:2, :])
+    ready(3)
+    cq[...] = dot_nn(norm_cross, wa[6]).astype(BF)
+    attention_forward(pairs, cq, mk, mv, pc, cc, allowed_cross)
+    part_out[1] = dot_nt(cc[...], wa[7]).astype(BF)
+    swap = exchange_start(1)
+    copies.save(wa, wa_o)
+    for src, dst in ((q, q_o), (k, k_o), (v, v_o), (sc, sc_o), (ps, ps_o), (mk, mk_o), (mv, mv_o), (cq, cq_o), (cc, cc_o), (pc, pc_o), (slots, sel_o), (one, one_o), (gain_sum, gain_o)):
+        copies.save(src, dst)
+    forward(4)
+    complete(4)
+    forward(5)
+    complete(5)
+    two[...] = one[...] + exchanged(1, swap)
+    copies.save(two, two_o)
+    norm_ff = rms_rows(two[...], gain_sum[2:3, :])
+    ready(4)
+    copies.save(wgu, wgu_o)
+    ga[...] = dot_nn(norm_ff, wgu[0]).astype(BF)
+    up[...] = dot_nn(norm_ff, wgu[1]).astype(BF)
+    copies.save(ga, ga_o)
+    copies.save(up, up_o)
+    ff_hidden = (smooth_gate(ga[...].astype(F32)) * up[...].astype(F32)).astype(BF)
+    ready(5)
+    copies.save(wd, wd_o)
+    part_out[2] = (
+        dot_nt(ff_hidden[:, :wide_cols], wd[0]) + dot_nt(ff_hidden[:, wide_cols:], wd[1])
+    ).astype(BF)
+    swap = exchange_start(2)
+    three[...] = two[...] + exchanged(2, swap)
+    block[...] = three[...].astype(BF)
+    exit_rows[...] = rms_rows(three[...], gain_sum[3:4, :])
+    copies.save(three, three_o)
+    copies.save(block, block_o)
+    copies.save(exit_rows, exit_o)
+    links.finish()
+    copies.finish()
+
+
+def forward_layer(layer_input, memory, group_map, lengths, gain_rows, weights):
+    count = group_map.shape[0]
+    rows, width = layer_input.shape
+    heads = weights[0].shape[1]
+    units = weights[8].shape[1]
+    slots = count * max(2, 2 * rows // count)
+    pairs = heads // (2 * HEAD_DIM)
+    kept = [
+        ((rows, width), BF), ((rows, width), F32), ((rows, width), F32), ((rows, width), F32), ((rows, width), BF),
+        ((rows, heads), BF), ((rows, heads), BF), ((rows, heads), BF), ((rows, heads), BF),
+        ((slots, heads), BF), ((slots, heads), BF), ((rows, heads), BF), ((rows, heads), BF),
+        ((pairs, 2 * rows, rows), BF), ((pairs, 2 * rows, slots), BF),
+        ((rows, units), BF), ((rows, units), BF), ((slots, width), BF),
+        ((8, width, heads), BF), ((2, width, units), BF), ((2, width, units // 2), BF), ((8, width), F32),
+    ]
+    vmem, hbm = pl.BlockSpec(memory_space=pltpu.VMEM), pl.BlockSpec(memory_space=pl.ANY)
+    scratch = [
+        pltpu.VMEM((8, width, heads), BF), pltpu.VMEM((2, width, units), BF), pltpu.VMEM((2, width, units // 2), BF),
+        pltpu.VMEM((count, 8, width), F32), pltpu.VMEM((slots, width), BF), pltpu.VMEM((slots, width), BF),
+        pltpu.VMEM((3, rows, width), BF), pltpu.VMEM((3, rows, width), BF),
+    ]
+    scratch += [pltpu.VMEM(shape, kind) for shape, kind in kept[:17]]
+    scratch += [pltpu.VMEM((8, width), F32)]
+    scratch += [pltpu.SemaphoreType.DMA((64,)), pltpu.SemaphoreType.DMA((64,)), pltpu.SemaphoreType.DMA((40,))]
+    return pl.pallas_call(
+        forward_kernel,
+        out_shape=[jax.ShapeDtypeStruct(shape, kind) for shape, kind in kept],
+        in_specs=[vmem, vmem, vmem, pl.BlockSpec(memory_space=pltpu.SMEM), vmem] + [hbm] * 11,
+        out_specs=[hbm] * len(kept),
+        scratch_shapes=scratch,
+        compiler_params=pltpu.CompilerParams(
+            collective_id=0, has_side_effects=True, vmem_limit_bytes=48 << 20
+        ),
+        name="forward_layer",
+    )(layer_input, memory, group_map, lengths, gain_rows, *weights)
+
+
+def saved_attend_backward(queries, keys, values, context_grad, probs):
+    factor = HEAD_DIM ** (-0.5)
+    rows = queries.shape[0]
+
+    def one_head(parts):
+        query, key_rows, value_rows, grad_rows, soft_bf = parts
+        soft = soft_bf.astype(jnp.float32)
+        soft_grad = project_back(grad_rows, value_rows)
+        score_grad = (soft * (soft_grad - jnp.sum(soft * soft_grad, axis=1, keepdims=True))).astype(
+            jnp.bfloat16
+        )
+        query_grad = project(score_grad, key_rows) * factor
+        key_grad = outer_rows(score_grad, query) * factor
+        value_grad = outer_rows(soft_bf, grad_rows)
+        return (query_grad, key_grad, value_grad)
+
+    grads = lax.map(
+        one_head,
+        (
+            split_heads(queries),
+            split_heads(keys),
+            split_heads(values),
+            split_heads(context_grad),
+            probs.reshape(-1, rows, probs.shape[2]),
+        ),
+    )
+    return (join_heads(grads[0]), join_heads(grads[1]), join_heads(grads[2]))
+
+
+def fused_body(
+    layer_input,
+    memory,
+    reader_map,
+    target_ids,
+    target_lengths,
+    out_grad,
+    self_q,
+    self_k,
+    self_v,
+    self_o,
+    cross_q,
+    cross_k,
+    cross_v,
+    cross_o,
+    ff_gate,
+    ff_up,
+    ff_out,
+    gain_self,
+    gain_cross,
+    gain_ff,
+    gain_exit,
+    exit_table,
+):
+    wide_count = lax.axis_size("wide")
+    wide_index = lax.axis_index("wide")
+    seq_rows = layer_input.shape[0]
+    group_index = lax.axis_index("grp")
+    group_lengths = lax.dynamic_slice_in_dim(target_lengths, group_index * wide_count, wide_count)
+    depth = gain_self.shape[0]
+    stacked = jnp.stack([gain_self, gain_cross, gain_ff, gain_exit]).astype(jnp.float32)
+    gain_rows = lax.dynamic_update_slice(
+        jnp.zeros((8, wide_count * depth), jnp.float32), stacked, (0, wide_index * depth)
+    )
+    (
+        block_output, resid_one, resid_two, resid_three, norm_exit, queries, keys, values, cross_queries,
+        keys_read, values_read, context_self, context_cross, probs_self, probs_cross, gate_act, up_act, slots,
+        attn_weights, gate_weights, down_weights, gains,
+    ) = forward_layer(
+        layer_input, memory, reader_map.reshape(wide_count, -1), target_lengths, gain_rows,
+        (self_q, self_k, self_v, self_o, cross_q, cross_k, cross_v, cross_o, ff_gate, ff_up, ff_out),
+    )
+    w_query, w_key, w_value, w_output, c_key, c_value, c_query, c_output = attn_weights
+    w_gate, w_up = gate_weights
+    w_down = jnp.concatenate([down_weights[0], down_weights[1]], axis=1)
+    gain_one, gain_two, gain_three, gain_last = gains[0], gains[1], gains[2], gains[3]
+    hidden = layer_input.astype(jnp.float32)
+    norm_self, unit_self, factor_self = normalize(hidden, gain_one)
+    rows_each = memory.shape[0]
+    capacity = max(2, 2 * rows_each // wide_count)
+    slot_count = wide_count * capacity
+    slot_valid, slot_target = read_slots(reader_map, wide_index, wide_count, rows_each, capacity)
+    read_table = (
+        jnp.zeros((slot_count,), jnp.int32)
+        .at[slot_target]
+        .set(lax.iota(jnp.int32, wide_count * rows_each), mode="drop")
+    )
+    norm_cross, unit_cross, factor_cross = normalize(resid_one, gain_two)
+    norm_ff, unit_ff, factor_ff = normalize(resid_two, gain_three)
+    up_float = up_act.astype(jnp.float32)
+    gelu_value, gelu_pull = jax.vjp(smooth_gate, gate_act.astype(jnp.float32))
+    ff_hidden = (gelu_value * up_float).astype(jnp.bfloat16)
+    unit_exit, factor_exit = normalize(resid_three, gain_last)[1:]
+    rows_all = lax.all_gather(norm_exit, "wide", axis=0, tiled=True)
+    group_tokens = rows_all.shape[0]
+    vocab_rows = exit_table.shape[0]
+    scale_exit = float(rows_all.shape[1]) ** (-0.5)
+    logits = project_back(rows_all, exit_table) * scale_exit
+    vocab_ids = lax.axis_index(("wide", "tp")) * vocab_rows + lax.iota(jnp.int32, vocab_rows)
+    is_target = target_ids[:, None] == vocab_ids[None, :]
+    local_high = jnp.max(logits, axis=1)
+    local_total = jnp.sum(jnp.exp(logits - local_high[:, None]), axis=1)
+    local_pick = jnp.sum(jnp.where(is_target, logits, 0.0), axis=1)
+    highest, total_exp, target_logit = merged(
+        (local_high, local_total, local_pick), ("wide", "tp"), merge_softmax
+    )
+    log_total = highest + jnp.log(total_exp)
+    token_place = lax.iota(jnp.int32, group_tokens)
+    valid = token_place % seq_rows < jnp.repeat(
+        group_lengths, seq_rows, total_repeat_length=group_tokens
+    )
+    token_count = jnp.sum(target_lengths).astype(jnp.float32)
+    token_weight = jnp.where(valid, 1.0, 0.0).astype(jnp.float32) / token_count
+    group_loss = jnp.sum(token_weight * (log_total - target_logit))
+    logit_grad = (
+        (jnp.exp(logits - log_total[:, None]) - jnp.where(is_target, 1.0, 0.0))
+        * token_weight[:, None]
+    ).astype(jnp.bfloat16)
+    rows_grad_all = project(logit_grad, exit_table) * scale_exit
+    exit_grad = outer_rows(logit_grad, rows_all) * scale_exit
+    rows_part = lax.psum_scatter(
+        rows_grad_all.astype(jnp.bfloat16), "wide", scatter_dimension=0, tiled=True
+    )
+    norm_exit_grad = lax.psum(rows_part, "tp").astype(jnp.float32)
+    gain_exit_grad, back_exit = normalize_back(
+        resid_three, unit_exit, factor_exit, gain_last, norm_exit_grad
+    )
+    resid_three_grad = out_grad.astype(jnp.float32) + back_exit
+    ff_branch = resid_three_grad.astype(jnp.bfloat16)
+    w_down_grad = outer_rows(ff_branch, ff_hidden)
+    hidden_grad = project(ff_branch, w_down)
+    gate_grad = gelu_pull(hidden_grad * up_float)[0].astype(jnp.bfloat16)
+    up_grad = (hidden_grad * gelu_value).astype(jnp.bfloat16)
+    w_gate_grad = outer_rows(norm_ff, gate_grad)
+    w_up_grad = outer_rows(norm_ff, up_grad)
+    norm_ff_grad = input_total(project_back(gate_grad, w_gate) + project_back(up_grad, w_up))
+    gain_ff_grad, back_ff = normalize_back(resid_two, unit_ff, factor_ff, gain_three, norm_ff_grad)
+    resid_two_grad = resid_three_grad + back_ff
+    cross_branch = resid_two_grad.astype(jnp.bfloat16)
+    c_output_grad = outer_rows(cross_branch, context_cross)
+    cross_context_grad = project(cross_branch, c_output).astype(jnp.bfloat16)
+    cross_query_grad, keys_grad_read, values_grad_read = saved_attend_backward(
+        cross_queries, keys_read, values_read, cross_context_grad, probs_cross
+    )
+    empty_grads = jnp.zeros((wide_count * rows_each, keys_grad_read.shape[1]), jnp.float32)
+    keys_grad_all = empty_grads.at[read_table].add(keys_grad_read)
+    values_grad_all = empty_grads.at[read_table].add(values_grad_read)
+    keys_grad, values_grad = (
+        lax.psum_scatter(
+            keys_grad_all.astype(jnp.bfloat16), "wide", scatter_dimension=0, tiled=True
+        ).astype(jnp.float32),
+        lax.psum_scatter(
+            values_grad_all.astype(jnp.bfloat16), "wide", scatter_dimension=0, tiled=True
+        ).astype(jnp.float32),
+    )
+    keys_grad = keys_grad.astype(jnp.bfloat16)
+    values_grad = values_grad.astype(jnp.bfloat16)
+    cross_query_grad = cross_query_grad.astype(jnp.bfloat16)
+    c_query_grad = outer_rows(norm_cross, cross_query_grad)
+    c_key_grad = outer_rows(memory, keys_grad)
+    c_value_grad = outer_rows(memory, values_grad)
+    norm_cross_grad, memory_grad = (
+        lax.psum(project_back(cross_query_grad, c_query).astype(jnp.bfloat16), "tp").astype(
+            jnp.float32
+        ),
+        lax.psum(
+            (project_back(keys_grad, c_key) + project_back(values_grad, c_value)).astype(
+                jnp.bfloat16
+            ),
+            "tp",
+        ).astype(jnp.float32),
+    )
+    gain_cross_grad, back_cross = normalize_back(
+        resid_one, unit_cross, factor_cross, gain_two, norm_cross_grad
+    )
+    resid_one_grad = resid_two_grad + back_cross
+    self_branch = resid_one_grad.astype(jnp.bfloat16)
+    w_output_grad = outer_rows(self_branch, context_self)
+    self_context_grad = project(self_branch, w_output).astype(jnp.bfloat16)
+    query_grad, key_grad, value_grad = saved_attend_backward(
+        queries, keys, values, self_context_grad, probs_self
+    )
+    query_grad = query_grad.astype(jnp.bfloat16)
+    key_grad = key_grad.astype(jnp.bfloat16)
+    value_grad = value_grad.astype(jnp.bfloat16)
+    w_query_grad = outer_rows(norm_self, query_grad)
+    w_key_grad = outer_rows(norm_self, key_grad)
+    w_value_grad = outer_rows(norm_self, value_grad)
+    norm_self_grad = input_total(
+        project_back(query_grad, w_query)
+        + project_back(key_grad, w_key)
+        + project_back(value_grad, w_value)
+    )
+    gain_self_grad, back_self = normalize_back(
+        hidden, unit_self, factor_self, gain_one, norm_self_grad
+    )
+    input_grad = resid_one_grad + back_self
+    shards = (
+        lax.psum_scatter(
+            w_query_grad.astype(jnp.bfloat16), "wide", scatter_dimension=0, tiled=True
+        ).astype(jnp.float32),
+        lax.psum_scatter(
+            w_key_grad.astype(jnp.bfloat16), "wide", scatter_dimension=0, tiled=True
+        ).astype(jnp.float32),
+        lax.psum_scatter(
+            w_value_grad.astype(jnp.bfloat16), "wide", scatter_dimension=0, tiled=True
+        ).astype(jnp.float32),
+        lax.psum_scatter(
+            w_output_grad.astype(jnp.bfloat16), "wide", scatter_dimension=0, tiled=True
+        ).astype(jnp.float32),
+        lax.psum_scatter(
+            c_query_grad.astype(jnp.bfloat16), "wide", scatter_dimension=0, tiled=True
+        ).astype(jnp.float32),
+        lax.psum_scatter(
+            c_key_grad.astype(jnp.bfloat16), "wide", scatter_dimension=0, tiled=True
+        ).astype(jnp.float32),
+        lax.psum_scatter(
+            c_value_grad.astype(jnp.bfloat16), "wide", scatter_dimension=0, tiled=True
+        ).astype(jnp.float32),
+        lax.psum_scatter(
+            c_output_grad.astype(jnp.bfloat16), "wide", scatter_dimension=0, tiled=True
+        ).astype(jnp.float32),
+        lax.psum_scatter(
+            w_gate_grad.astype(jnp.bfloat16), "wide", scatter_dimension=0, tiled=True
+        ).astype(jnp.float32),
+        lax.psum_scatter(
+            w_up_grad.astype(jnp.bfloat16), "wide", scatter_dimension=0, tiled=True
+        ).astype(jnp.float32),
+        lax.psum_scatter(
+            w_down_grad.astype(jnp.bfloat16), "wide", scatter_dimension=0, tiled=True
+        ).astype(jnp.float32),
+        lax.psum_scatter(
+            gain_self_grad.astype(jnp.bfloat16), "wide", scatter_dimension=0, tiled=True
+        ).astype(jnp.float32),
+        lax.psum_scatter(
+            gain_cross_grad.astype(jnp.bfloat16), "wide", scatter_dimension=0, tiled=True
+        ).astype(jnp.float32),
+        lax.psum_scatter(
+            gain_ff_grad.astype(jnp.bfloat16), "wide", scatter_dimension=0, tiled=True
+        ).astype(jnp.float32),
+        lax.psum_scatter(
+            gain_exit_grad.astype(jnp.bfloat16), "wide", scatter_dimension=0, tiled=True
+        ).astype(jnp.float32),
+    )
+    totals = (
+        lax.psum(shards[0].astype(jnp.bfloat16), "grp").astype(jnp.float32),
+        lax.psum(shards[1].astype(jnp.bfloat16), "grp").astype(jnp.float32),
+        lax.psum(shards[2].astype(jnp.bfloat16), "grp").astype(jnp.float32),
+        lax.psum(shards[3].astype(jnp.bfloat16), "grp").astype(jnp.float32),
+        lax.psum(shards[4].astype(jnp.bfloat16), "grp").astype(jnp.float32),
+        lax.psum(shards[5].astype(jnp.bfloat16), "grp").astype(jnp.float32),
+        lax.psum(shards[6].astype(jnp.bfloat16), "grp").astype(jnp.float32),
+        lax.psum(shards[7].astype(jnp.bfloat16), "grp").astype(jnp.float32),
+        lax.psum(shards[8].astype(jnp.bfloat16), "grp").astype(jnp.float32),
+        lax.psum(shards[9].astype(jnp.bfloat16), "grp").astype(jnp.float32),
+        lax.psum(shards[10].astype(jnp.bfloat16), "grp").astype(jnp.float32),
+        lax.psum(shards[11].astype(jnp.bfloat16), "grp").astype(jnp.float32),
+        lax.psum(shards[12].astype(jnp.bfloat16), "grp").astype(jnp.float32),
+        lax.psum(shards[13].astype(jnp.bfloat16), "grp").astype(jnp.float32),
+        lax.psum(shards[14].astype(jnp.bfloat16), "grp").astype(jnp.float32),
+        lax.psum(exit_grad.astype(jnp.bfloat16), "grp").astype(jnp.float32),
+        lax.psum(group_loss.astype(jnp.bfloat16), "grp").astype(jnp.float32),
+    )
+    return (
+        block_output,
+        totals[16],
+        input_grad,
+        memory_grad,
+        totals[0],
+        totals[1],
+        totals[2],
+        totals[3],
+        totals[4],
+        totals[5],
+        totals[6],
+        totals[7],
+        totals[8],
+        totals[9],
+        totals[10],
+        totals[11],
+        totals[12],
+        totals[13],
+        totals[14],
+        totals[15],
+    )
+
+
+def fits(mesh):
+    return mesh.shape["wide"] == 4 and mesh.shape["tp"] == 2 and mesh.shape["grp"] == 4
+
+
 def solution(mesh):
     placed = (
         P(("grp", "wide"), None),
@@ -464,7 +1127,7 @@
         P(("wide", "tp"), None),
     )
     return jax.shard_map(
-        body,
+        fused_body if fits(mesh) else plain_body,
         mesh=mesh,
         in_specs=placed,
         out_specs=(

time: 1320 us -> 1050 us (0.80)
  blocking collectives: 219 us -> 73.7 us
  waiting for transfers between devices: 693 us -> 577 us
  Pallas kernels: 0 us -> 114 us
  matrix products: 177 us -> 123 us
  other arithmetic: 124 us -> 78.5 us
    all_gather x10 -> x0, blocking collectives: 136 us -> none  [the longest x1 16.5 us: body(): lax.all_gather(memory_keys, 'wide', axis=0, tiled=True)]
    pallas_call x0 -> x1, Pallas kernels: none -> 114 us  [forward_layer(): pl.pallas_call(forward_kernel, out_shape=[jax.ShapeDtypeStruct(shape, kin...]
    psum x6 -> x3, waiting for transfers between devices: 257 us -> 183 us  [the longest x1 142 us: fused_body(): lax.psum(shards[5].astype(jnp.bfloat16), 'grp').astype(jnp.float32)]
    all_gather x4 -> x1, waiting for transfers between devices: 105 us -> 34.9 us  [fused_body(): rows_all = lax.all_gather(norm_exit, 'wide', axis=0, tiled=True)]
    psum x2, waiting for transfers between devices: 25.8 us -> 61.8 us  [input_total(): return lax.psum(partial_rows.astype(jnp.bfloat16), 'tp').astype(jnp.float32)]
    lt x13 -> x0, other arithmetic: 31.5 us -> none  [the longest x12 30.3 us: read_slots(): place % capacity]
    dot_general x36 -> x16, matrix products: 53 us -> 24.1 us  [project(): return jnp.dot(left, right, preferred_element_type=jnp.float32)]
    dot_general x48 -> x21, matrix products: 65.6 us -> 36.7 us  [project_back(): lax.dot_general(left, right, (((1,), (1,)), ((), ())), preferred_element_...]
  transfers between devices with their start and end apart: 26 -> 20, of which waited for: 20 -> 17; matrix products, arithmetic and copies ran while one was open for 9% -> 11% of each run, Pallas kernels for 0% -> 0%
where the time goes in v1:
time: 1050 us; the launch traced here: 1040 us
  waiting for transfers between devices  577 us (55%)
  matrix products  123 us (12%)
  Pallas kernels  114 us (11%)
  other arithmetic  78.5 us (7%)
  blocking collectives  73.7 us (7%)
  local copies, waits for them, and re-layouts  55.5 us (5%)
  between operations  18.6 us (2%)
    psum x1, waiting for transfers between devices, fused_body(): lax.psum(shards[5].astype(jnp.bfloat16), 'grp').astype(jnp.float32)  142 us
    pallas_call x1, Pallas kernels, forward_layer(): pl.pallas_call(forward_kernel, out_shape=[jax.ShapeDtypeStruct(shape, kin...  114 us
    dot_general x36, matrix products, outer_rows(): lax.dot_general(left, right, (((0,), (0,)), ((), ())), preferred_element_...  61.9 us
    psum x2, waiting for transfers between devices, input_total(): return lax.psum(partial_rows.astype(jnp.bfloat16), 'tp').astype(jnp.float32)  61.8 us
    all_gather x3, blocking collectives, merged(): lax.all_gather(part.astype(kind), axis)  58.3 us
    reduce_scatter x1, waiting for transfers between devices, fused_body(): lax.psum_scatter(rows_grad_all.astype(jnp.bfloat16), 'wide', scatter_dime...  42.9 us
    reduce_scatter x1, waiting for transfers between devices, fused_body(): lax.psum_scatter(w_down_grad.astype(jnp.bfloat16), 'wide', scatter_dimens...  38.6 us
    dot_general x21, matrix products, project_back(): lax.dot_general(left, right, (((1,), (1,)), ((), ())), preferred_element_...  36.7 us
  transfers between devices with their start and end apart: 20, of which 17 were waited for; matrix products, arithmetic and copies ran while one was open for 11% of the time, Pallas kernels for 0%

profile of v1, /device:TPU:19, one launch (start us, length us, event | category | flops | bytes accessed | tf_op | source)
XLA Modules:
  0.0 1043.0 jit_solution(1438263799467705634)
XLA Ops:
  24.0 114.2 %forward_layer.1 = (bf16[256,768]{1,0:T(8,128)(2,1)S(1)}, f32[256,768]{1,0:T(8,128)}, f32[256,768]{1,0:T(8,128)}, f32[256,768]{1,0:T(8,128)}, bf16[256,768]{1,0:...) custom-call(bf16[256,768]{1,0:T(8,128)(2,1)S(1)} %copy-done, ...), custom_call_target="tpu_custom_call" | custom-call | tf_op jit(solution)/shard_map/forward_layer/pallas_call | solution.py:801
  140.6 34.9 %all-gather.5.cloned.1.call-done = bf16[1024,768]{1,0:T(8,128)(2,1)} async-done(((bf16[256,768]{1,0:T(8,128)(2,1)}), bf16[1024,768]{1,0:T(8,128)(2,1)}) %all-gather.5.cloned.1.call-update) | async-done | bytes 1572880 | tf_op jit(solution)/shard_map/all_gather | solution.py:906
  175.5 9.4 multiply_reduce_fusion
  190.6 17.0 %all-gather.2 = bf16[8192]{0:T(1024)(128)(2,1)S(1)} all-gather(bf16[1024]{0:T(1024)(128)(2,1)S(1)} %get-tuple-element.464), channel_id=4, replica_groups=mesh['grp'=4,'wide'=4,'tp'=2] {'wide','tp'}, dimensions={0}, use_global_device_ids=true | all-gather | bytes 18432 | tf_op jit(solution)/shard_map/all_gather | solution.py:17
  207.6 20.5 %all-gather.1 = bf16[8192]{0:T(1024)(128)(2,1)S(1)} all-gather(bf16[1024]{0:T(1024)(128)(2,1)S(1)} %get-tuple-element.465), channel_id=3, replica_groups=mesh['grp'=4,'wide'=4,'tp'=2] {'wide','tp'}, dimensions={0}, use_global_device_ids=true | all-gather | bytes 18432 | tf_op jit(solution)/shard_map/all_gather | solution.py:17
  228.1 20.8 %all-gather = bf16[8192]{0:T(1024)(128)(2,1)S(1)} all-gather(bf16[1024]{0:T(1024)(128)(2,1)S(1)} %convert_element_type.396), channel_id=2, replica_groups=mesh['grp'=4,'wide'=4,'tp'=2] {'wide','tp'}, dimensions={0}, use_global_device_ids=true | all-gather | bytes 18432 | tf_op jit(solution)/shard_map/all_gather | solution.py:17
  252.8 8.4 fusion.50
  264.6 10.8 %multiply_convert_fusion.1 = bf16[1024,768]{1,0:T(8,128)(2,1)} fusion(bf16[1024,4016]{0,1:T(8,128)(2,1)S(1)} %fusion.50, bf16[4016,768]{1,0:T(8,128)(2,1)} %param.51), kind=kOutput, calls=%fused_computation.74 | convolution fusion | flops 6318194688 | bytes 15966208 | tf_op jit(solution)/shard_map/dot_general | solution.py:31
  285.0 42.9 %reduce-scatter.19.cloned.1.call-done = bf16[256,768]{1,0:T(8,128)(2,1)} async-done(((bf16[1024,768]{1,0:T(8,128)(2,1)}), bf16[256,768]{1,0:T(8,128)(2,1)}) %reduce-scatter.19.cloned.1.call-update) | async-done | bytes 393232 | tf_op jit(solution)/shard_map/reduce_scatter | solution.py:933
  330.9 24.2 %all-reduce.14.cloned.1.call-done = bf16[256,768]{1,0:T(8,128)(2,1)} async-done(((bf16[256,768]{1,0:T(8,128)(2,1)}), bf16[256,768]{1,0:T(8,128)(2,1)}) %all-reduce.14.cloned.1.call-update) | async-done | bytes 393232 | tf_op jit(solution)/shard_map/psum | solution.py:936
  364.2 25.8 %all-reduce.16.cloned.1.call-done = bf16[256,768]{1,0:T(8,128)(2,1)} async-done(((bf16[256,768]{1,0:T(8,128)(2,1)}), bf16[256,768]{1,0:T(8,128)(2,1)}) %all-reduce.16.cloned.1.call-update) | async-done | bytes 393232 | tf_op jit(solution)/shard_map/psum | solution.py:134
  395.6 36.4 %while.49 = (s32[]{:T(128)}, bf16[6,256,64]{1,2,0:T(8,128)(2,1)S(1)}, f32[6,512,64]{1,2,0:T(8,128)}, f32[6,512,64]{1,2,0:T(8,128)}, bf16[6,256,512]{2,1,0:T(8,12...) while((s32[]{:T(128)}, ...), condition=%wide.region_18.19_spmd, body=%wide.region_16.18_spmd.sunk | while | flops 68075264 | bytes 3185769 | solution.py:830
  434.4 5.9 scatter_custom_fusion.1
  445.0 5.9 scatter_custom_fusion.2
  455.9 8.3 reduce-scatter.21.cloned.1.call-done
  466.7 22.9 %reduce-scatter.23.cloned.1.call-done = bf16[256,384]{1,0:T(8,128)(2,1)} async-done(((bf16[1024,384]{1,0:T(8,128)(2,1)}), bf16[256,384]{1,0:T(8,128)(2,1)}) %reduce-scatter.23.cloned.1.call-update) | async-done | bytes 196624 | tf_op jit(solution)/shard_map/reduce_scatter | solution.py:964
  502.2 16.9 %all-reduce.18.cloned.1.call-done = bf16[256,768]{1,0:T(8,128)(2,1)} async-done(((bf16[256,768]{1,0:T(8,128)(2,1)}), bf16[256,768]{1,0:T(8,128)(2,1)}) %all-reduce.18.cloned.1.call-update) | async-done | bytes 393232 | tf_op jit(solution)/shard_map/psum | solution.py:975
  527.5 25.5 %while.50 = (s32[]{:T(128)}, bf16[6,256,64]{1,2,0:T(8,128)(2,1)S(1)}, bf16[6,256,64]{1,2,0:T(8,128)(2,1)S(1)}, bf16[6,256,64]{1,2,0:T(8,128)(2,1)S(1)}, bf16[6,2...) while((s32[]{:T(128)}, ...), condition=%wide.region_24.25_spmd, body=%wide.region_22.24_spmd.sunk | while | flops 34045696 | bytes 2202217 | solution.py:830
  575.2 11.2 %multiply_convert_fusion = bf16[4016,768]{1,0:T(8,128)(2,1)} fusion(bf16[1024,4016]{0,1:T(8,128)(2,1)} %copy-done.22, bf16[1024,768]{1,0:T(8,128)(2,1)} %all-gather.5.cloned.1.call-done), kind=kOutput, calls=%fused_computation.73 | convolution fusion | flops 6322790400 | bytes 15966208 | tf_op jit(solution)/shard_map/dot_general | solution.py:41
  589.9 20.5 %reduce-scatter.35.cloned.1.call-done = bf16[192,384]{1,0:T(8,128)(2,1)} async-done(((bf16[768,384]{1,0:T(8,128)(2,1)}), bf16[192,384]{1,0:T(8,128)(2,1)}) %reduce-scatter.35.cloned.1.call-update) | async-done | bytes 147472 | tf_op jit(solution)/shard_map/reduce_scatter | solution.py:1032
  610.3 22.6 %reduce-scatter.31.cloned.1.call-done = bf16[192,384]{1,0:T(8,128)(2,1)} async-done(((bf16[768,384]{1,0:T(8,128)(2,1)}), bf16[192,384]{1,0:T(8,128)(2,1)}) %reduce-scatter.31.cloned.1.call-update) | async-done | bytes 147472 | tf_op jit(solution)/shard_map/reduce_scatter | solution.py:1020
  632.9 22.7 %reduce-scatter.29.cloned.1.call-done = bf16[192,384]{1,0:T(8,128)(2,1)} async-done(((bf16[768,384]{1,0:T(8,128)(2,1)}), bf16[192,384]{1,0:T(8,128)(2,1)}) %reduce-scatter.29.cloned.1.call-update) | async-done | bytes 147472 | tf_op jit(solution)/shard_map/reduce_scatter | solution.py:1017
  655.7 22.6 %reduce-scatter.27.cloned.1.call-done = bf16[192,384]{1,0:T(8,128)(2,1)} async-done(((bf16[768,384]{1,0:T(8,128)(2,1)}), bf16[192,384]{1,0:T(8,128)(2,1)}) %reduce-scatter.27.cloned.1.call-update) | async-done | bytes 147472 | tf_op jit(solution)/shard_map/reduce_scatter | solution.py:1014
  678.3 23.1 %reduce-scatter.25.cloned.1.call-done = bf16[192,384]{1,0:T(8,128)(2,1)} async-done(((bf16[768,384]{1,0:T(8,128)(2,1)}), bf16[192,384]{1,0:T(8,128)(2,1)}) %reduce-scatter.25.cloned.1.call-update) | async-done | bytes 147472 | tf_op jit(solution)/shard_map/reduce_scatter | solution.py:1011
  701.4 38.6 %reduce-scatter.41.cloned.1.call-done = bf16[192,1024]{1,0:T(8,128)(2,1)} async-done(((bf16[768,1024]{1,0:T(8,128)(2,1)}), bf16[192,1024]{1,0:T(8,128)(2,1)}) %reduce-scatter.41.cloned.1.call-update) | async-done | bytes 393232 | tf_op jit(solution)/shard_map/reduce_scatter | solution.py:1041
  740.0 36.6 %reduce-scatter.39.cloned.1.call-done = bf16[192,1024]{1,0:T(8,128)(2,1)} async-done(((bf16[768,1024]{1,0:T(8,128)(2,1)}), bf16[192,1024]{1,0:T(8,128)(2,1)}) %reduce-scatter.39.cloned.1.call-update) | async-done | bytes 393232 | tf_op jit(solution)/shard_map/reduce_scatter | solution.py:1038
  776.5 36.6 %reduce-scatter.37.cloned.1.call-done = bf16[192,1024]{1,0:T(8,128)(2,1)} async-done(((bf16[768,1024]{1,0:T(8,128)(2,1)}), bf16[192,1024]{1,0:T(8,128)(2,1)}) %reduce-scatter.37.cloned.1.call-update) | async-done | bytes 393232 | tf_op jit(solution)/shard_map/reduce_scatter | solution.py:1035
  814.4 35.9 %all-reduce.22.cloned.1.call-done = (bf16[256,768]{1,0:T(8,128)(2,1)}, bf16[256,768]{1,0:T(8,128)(2,1)}) async-done(((bf16[256,768]{1,0:T(8,128)(2,1)}, bf16[256,768]{1,0:T(8,128)(2,1)}), (bf16[256,768]{1,0:T(8,128)(2,1)}, bf16[256,768]{1,0:T(8,128)(2,1)})) %all-reduce.22.cloned.1.call-update) | async-done | bytes 786448 | tf_op jit(solution)/shard_map/psum | solution.py:134
  851.7 7.0 all-reduce.4
  859.0 8.4 all-reduce.5
  874.4 141.8 %all-reduce.20.cloned.1.call-done = (bf16[192,384]{0,1:T(8,128)(2,1)}, bf16[192,384]{0,1:T(8,128)(2,1)}, bf16[192,384]{1,0:T(8,128)(2,1)}, bf16[192,384]{1,0:T(8...) async-done(((bf16[192,384]{0,1:T(8,128)(2,1)}, ...) | async-done | bytes 8527888 | tf_op jit(solution)/shard_map/psum | solution.py:1063
  1016.3 8.5 convert_element_type.486
  (382 shorter events, 199.4 us)
Async XLA Ops:
  7.2 168.3 %all-gather.5.cloned.1.call-start = ((), (), s32[]{:S(2)}) async-start(), calls=%async_computation.14 | async-start | bytes 1966080 | tf_op jit(solution)/shard_map/all_gather | solution.py:906
  138.1 189.8 %reduce-scatter.19.cloned.1.call-start = ((), (), s32[]{:S(2)}) async-start(), calls=%async_computation.15 | async-start | bytes 1966080 | tf_op jit(solution)/shard_map/reduce_scatter | solution.py:933
  140.6 44.3 %copy-start.46 = (s32[1024]{0:T(1024)S(1)}, s32[1024]{0:T(1024)}, u32[]{:S(2)}) copy-start(s32[1024]{0:T(1024)} %param.33) | copy-start | bytes 12292
  184.9 64.7 %copy-start.50 = (pred[1024]{0:T(1024)(128)(4,1)S(1)}, pred[1024]{0:T(1024)(128)(4,1)}, u32[]{:S(2)}) copy-start(pred[1024]{0:T(1024)(128)(4,1)} %constant.276) | copy-start | bytes 3076
  185.0 64.7 %copy-start.51 = (pred[1024]{0:T(1024)(128)(4,1)S(1)}, pred[1024]{0:T(1024)(128)(4,1)}, u32[]{:S(2)}) copy-start(pred[1024]{0:T(1024)(128)(4,1)} %constant.277) | copy-start | bytes 3076
  185.0 64.7 %copy-start.52 = (pred[1024]{0:T(1024)(128)(4,1)S(1)}, pred[1024]{0:T(1024)(128)(4,1)}, u32[]{:S(2)}) copy-start(pred[1024]{0:T(1024)(128)(4,1)} %constant.278) | copy-start | bytes 3076
  275.5 79.6 %all-reduce.14.cloned.1.call-start = ((), (), s32[]{:S(2)}) async-start(), calls=%async_computation.16 | async-start | bytes 786432 | tf_op jit(solution)/shard_map/psum | solution.py:936
  277.4 77.6 %copy-start.23 = (f32[256,768]{1,0:T(8,128)S(1)}, f32[256,768]{1,0:T(8,128)}, u32[]{:S(2)}) copy-start(f32[256,768]{1,0:T(8,128)} %get-tuple-element.334) | copy-start | bytes 2359300
  328.0 62.0 %all-reduce.16.cloned.1.call-start = ((), (), s32[]{:S(2)}) async-start(), calls=%async_computation.17 | async-start | bytes 786432 | tf_op jit(solution)/shard_map/psum | solution.py:134
  362.7 29.1 %copy-start.25 = (f32[256,768]{1,0:T(8,128)S(1)}, f32[256,768]{1,0:T(8,128)}, u32[]{:S(2)}) copy-start(f32[256,768]{1,0:T(8,128)} %copy-done.24) | copy-start | bytes 2359300
  364.1 100.2 %reduce-scatter.21.cloned.1.call-start = ((), (), s32[]{:S(2)}) async-start(), calls=%async_computation.19 | async-start | bytes 983040 | tf_op jit(solution)/shard_map/reduce_scatter | solution.py:961
  442.7 46.9 %reduce-scatter.23.cloned.1.call-start = ((), (), s32[]{:S(2)}) async-start(), calls=%async_computation.20 | async-start | bytes 983040 | tf_op jit(solution)/shard_map/reduce_scatter | solution.py:964
  453.4 65.8 %all-reduce.18.cloned.1.call-start = ((), (), s32[]{:S(2)}) async-start(), calls=%async_computation.18 | async-start | bytes 786432 | tf_op jit(solution)/shard_map/psum | solution.py:975
  455.7 130.7 %reduce-scatter.43.cloned.1.call-start = ((), (), s32[]{:S(2)}) async-start(), calls=%async_computation.30 | async-start | bytes 737280
  465.5 34.1 %copy-start.1 = (bf16[256,768]{1,0:T(8,128)(2,1)S(1)}, bf16[256,768]{1,0:T(8,128)(2,1)}, u32[]{:S(2)}) copy-start(bf16[256,768]{1,0:T(8,128)(2,1)} %x_ref.1) | copy-start | bytes 1179652
  466.6 121.5 %reduce-scatter.45.cloned.1.call-start = ((), (), s32[]{:S(2)}) async-start(), calls=%async_computation.31 | async-start | bytes 737280
  493.9 96.0 %reduce-scatter.33.cloned.1.call-start = ((), (), s32[]{:S(2)}) async-start(), calls=%async_computation.25 | async-start | bytes 737280 | tf_op jit(solution)/shard_map/reduce_scatter | solution.py:1023
  497.8 112.6 %reduce-scatter.35.cloned.1.call-start = ((), (), s32[]{:S(2)}) async-start(), calls=%async_computation.26 | async-start | bytes 737280 | tf_op jit(solution)/shard_map/reduce_scatter | solution.py:1032
  502.2 130.7 %reduce-scatter.31.cloned.1.call-start = ((), (), s32[]{:S(2)}) async-start(), calls=%async_computation.24 | async-start | bytes 737280 | tf_op jit(solution)/shard_map/reduce_scatter | solution.py:1020
  527.4 128.3 %reduce-scatter.29.cloned.1.call-start = ((), (), s32[]{:S(2)}) async-start(), calls=%async_computation.23 | async-start | bytes 737280 | tf_op jit(solution)/shard_map/reduce_scatter | solution.py:1017
  554.4 123.9 %reduce-scatter.27.cloned.1.call-start = ((), (), s32[]{:S(2)}) async-start(), calls=%async_computation.22 | async-start | bytes 737280 | tf_op jit(solution)/shard_map/reduce_scatter | solution.py:1014
  555.8 145.6 %reduce-scatter.25.cloned.1.call-start = ((), (), s32[]{:S(2)}) async-start(), calls=%async_computation.21 | async-start | bytes 737280 | tf_op jit(solution)/shard_map/reduce_scatter | solution.py:1011
  557.2 182.7 %reduce-scatter.41.cloned.1.call-start = ((), (), s32[]{:S(2)}) async-start(), calls=%async_computation.29 | async-start | bytes 1966080 | tf_op jit(solution)/shard_map/reduce_scatter | solution.py:1041
  560.5 216.0 %reduce-scatter.39.cloned.1.call-start = ((), (), s32[]{:S(2)}) async-start(), calls=%async_computation.28 | async-start | bytes 1966080 | tf_op jit(solution)/shard_map/reduce_scatter | solution.py:1038
  564.0 249.1 %reduce-scatter.37.cloned.1.call-start = ((), (), s32[]{:S(2)}) async-start(), calls=%async_computation.27 | async-start | bytes 1966080 | tf_op jit(solution)/shard_map/reduce_scatter | solution.py:1035
  566.0 284.3 %all-reduce.22.cloned.1.call-start = ((), (), s32[]{:S(2)}) async-start(), calls=%async_computation.33 | async-start | bytes 1572864 | tf_op jit(solution)/shard_map/psum | solution.py:134
  574.9 441.3 %all-reduce.20.cloned.1.call-start = ((), (), s32[]{:S(2)}) async-start(), calls=%async_computation.32 | async-start | bytes 17252352 | tf_op jit(solution)/shard_map/psum | solution.py:1063
  586.4 226.7 %copy-start.55 = (u32[32]{0:T(128)S(1)}, u32[32]{0:T(128)}, u32[]{:S(2)}) copy-start(u32[32]{0:T(128)} %constant.283) | copy-start | bytes 388
  813.1 38.6 %copy-start.47 = (bf16[768]{0:T(1024)(128)(2,1)S(1)}, bf16[768]{0:T(1024)(128)(2,1)}, u32[]{:S(2)}) copy-start(bf16[768]{0:T(1024)(128)(2,1)} %get-tuple-element.466) | copy-start | bytes 4612
  813.1 38.6 %copy-start.48 = (bf16[768]{0:T(1024)(128)(2,1)S(1)}, bf16[768]{0:T(1024)(128)(2,1)}, u32[]{:S(2)}) copy-start(bf16[768]{0:T(1024)(128)(2,1)} %get-tuple-element.468) | copy-start | bytes 4612
  813.1 38.6 %copy-start.49 = (bf16[768]{0:T(1024)(128)(2,1)S(1)}, bf16[768]{0:T(1024)(128)(2,1)}, u32[]{:S(2)}) copy-start(bf16[768]{0:T(1024)(128)(2,1)} %get-tuple-element.470) | copy-start | bytes 4612
  813.1 59.1 %copy-start.20 = (f32[256,768]{1,0:T(8,128)S(1)}, f32[256,768]{1,0:T(8,128)}, u32[]{:S(2)}) copy-start(f32[256,768]{1,0:T(8,128)} %copy-done.19) | copy-start | bytes 2359300
  (45 other events, 284.4 us)
Sparse Core Ops, SparseCore 0:
  138.3 37.1 all-gather.4
  275.6 52.3 reduce-scatter.18
  330.3 24.7 all-reduce.13
  364.2 25.7 all-reduce.15
  442.8 21.4 reduce-scatter.20
  467.0 22.5 reduce-scatter.22
  492.4 26.6 all-reduce.17
  522.1 19.5 reduce-scatter.42
  544.7 20.2 reduce-scatter.44
  567.2 20.2 reduce-scatter.32
  589.9 20.3 reduce-scatter.34
  612.6 20.3 reduce-scatter.30
  635.3 20.3 reduce-scatter.28
  657.9 20.3 reduce-scatter.26
  681.1 20.2 reduce-scatter.24
  703.7 36.2 reduce-scatter.40
  742.2 34.2 reduce-scatter.38
  778.8 34.2 reduce-scatter.36
  816.7 33.5 all-reduce.21
  854.6 161.5 all-reduce.19

commit v2 on v0

--- a/solution.py
+++ b/solution.py
@@ -1,6 +1,11 @@
+import functools
+import types
+
 import jax
 import jax.numpy as jnp
 from jax import lax
+from jax.experimental import pallas as pl
+from jax.experimental.pallas import tpu as pltpu
 from jax.sharding import PartitionSpec as P
 
 HEAD_DIM = 64
@@ -138,7 +143,7 @@
     return (highest, total, first[2] + second[2])
 
 
-def body(
+def plain_body(
     layer_input,
     memory,
     reader_map,
@@ -438,6 +443,1107 @@
     )
 
 
+MESH = pl.DeviceIdType.MESH
+BF = jnp.bfloat16
+F32 = jnp.float32
+VMEM_BYTES = 63 << 20
+
+
+def dot_nn(left, right):
+    return lax.dot_general(left, right, (((1,), (0,)), ((), ())), preferred_element_type=F32)
+
+
+def dot_nt(left, right):
+    return lax.dot_general(left, right, (((1,), (1,)), ((), ())), preferred_element_type=F32)
+
+
+def dot_tn(left, right):
+    return lax.dot_general(left, right, (((0,), (0,)), ((), ())), preferred_element_type=F32)
+
+
+class Move:
+    def __init__(self, out, arrival):
+        self.out, self.arrival = out, arrival
+
+    def start(self):
+        self.out.start()
+        return self
+
+    def sent(self):
+        self.out.wait_send()
+
+    def landed(self):
+        self.arrival.wait_recv()
+
+
+class Links:
+    def __init__(self, send_sems, recv_sems):
+        self.send_sems, self.recv_sems = send_sems, recv_sems
+        self.used = 0
+        self.moves = []
+
+    def move(self, src, dst, device, lands):
+        k = self.used
+        self.used += 1
+        out = pltpu.make_async_remote_copy(
+            src_ref=src, dst_ref=dst, send_sem=self.send_sems.at[k], recv_sem=self.recv_sems.at[k],
+            device_id=device, device_id_type=MESH,
+        )
+        arrival = pltpu.make_async_remote_copy(
+            src_ref=lands, dst_ref=lands, send_sem=self.send_sems.at[k], recv_sem=self.recv_sems.at[k],
+            device_id=device, device_id_type=MESH,
+        )
+        made = Move(out, arrival)
+        self.moves.append(made)
+        return made
+
+    def finish(self):
+        for made in self.moves:
+            made.sent()
+
+    def finish_rest(self, done):
+        for made in self.moves:
+            if made not in done:
+                made.sent()
+
+
+class Copies:
+    def __init__(self, sems):
+        self.sems, self.used, self.pending = sems, 0, []
+
+    def start(self, src, dst):
+        made = pltpu.make_async_copy(src, dst, self.sems.at[self.used])
+        self.used += 1
+        made.start()
+        return made
+
+    def save(self, src, dst):
+        self.pending.append(self.start(src, dst))
+
+    def finish(self):
+        for made in self.pending:
+            made.wait()
+
+
+def greet(devices):
+    barrier = pltpu.get_barrier_semaphore()
+    for device in devices:
+        pl.semaphore_signal(barrier, inc=1, device_id=device, device_id_type=MESH)
+    pl.semaphore_wait(barrier, len(devices))
+
+
+def position(count):
+    g, w, t = lax.axis_index("grp"), lax.axis_index("wide"), lax.axis_index("tp")
+    c = lax.rem(g, 2)
+    left, right, far = (lax.rem(w + d, count) for d in (count - 1, 1, 2))
+    return types.SimpleNamespace(
+        count=count, g=g, w=w, t=t, c=c, yy=lax.div(g, 2), left=left, right=right, far=far,
+        to_left={"wide": left}, to_right={"wide": right}, to_far={"wide": far},
+        to_core={"grp": g + 1 - 2 * c}, to_y={"grp": lax.rem(g + 2, 4)}, to_tp={"tp": 1 - t},
+    )
+
+
+def rms_rows(values, gain):
+    factor = lax.rsqrt(jnp.mean(values * values, axis=1, keepdims=True) + EPSILON)
+    return (values * factor * gain).astype(BF)
+
+
+def lane_masks():
+    lane = lax.broadcasted_iota(jnp.int32, (1, 2 * HEAD_DIM), 1)
+    low = jnp.where(lane < HEAD_DIM, 1.0, 0.0).astype(F32)
+    return low.astype(BF), (1.0 - low).astype(BF)
+
+
+def both_heads(pair):
+    low, high = lane_masks()
+    return jnp.concatenate([pair * low, pair * high], axis=0)
+
+
+def pick_heads(stacked):
+    rows = stacked.shape[0] // 2
+    lane = lax.broadcasted_iota(jnp.int32, (rows, 2 * HEAD_DIM), 1)
+    return jnp.where(lane < HEAD_DIM, stacked[:rows], stacked[rows:])
+
+
+def pair_columns(p):
+    return pl.ds(pl.multiple_of(p * 2 * HEAD_DIM, 2 * HEAD_DIM), 2 * HEAD_DIM)
+
+
+def attention_forward(pairs, queries, keys, values, probs, context, allowed):
+    factor = HEAD_DIM ** (-0.5)
+
+    def step(p, carry):
+        cols = pair_columns(p)
+        scores = dot_nt(both_heads(queries[:, cols]), keys[:, cols]) * factor
+        scores = jnp.where(allowed, scores, MASKED)
+        exponent = jnp.exp(scores - jnp.max(scores, axis=1, keepdims=True))
+        soft = (exponent / jnp.sum(exponent, axis=1, keepdims=True)).astype(BF)
+        probs[p] = soft
+        context[:, cols] = pick_heads(dot_nn(soft, values[:, cols])).astype(BF)
+        return carry
+
+    lax.fori_loop(0, pairs, step, 0)
+
+
+def slot_choice(own_map, slots, count):
+    rows = own_map.shape[1]
+    capacity = slots // count
+    reader_iota = lax.broadcasted_iota(jnp.int32, (max(8, count), rows), 0)
+    matched = jnp.where(reader_iota == own_map, 1.0, 0.0).astype(F32)
+    before = lax.broadcasted_iota(jnp.int32, (rows, rows), 0) < lax.broadcasted_iota(jnp.int32, (rows, rows), 1)
+    ranks = dot_nn(matched.astype(BF), jnp.where(before, 1.0, 0.0).astype(BF))
+    rank = jnp.sum(matched * ranks, axis=0, keepdims=True).astype(jnp.int32)
+    slot_iota = lax.broadcasted_iota(jnp.int32, (slots, rows), 0)
+    return jnp.where(slot_iota == own_map * capacity + rank, 1.0, 0.0).astype(BF)
+
+
+class Gather:
+    def __init__(self, here, links, buf, first, depth, placed):
+        self.here, self.links, self.buf, self.placed = here, links, buf, placed
+        self.mine, self.other = first + here.c, first + 1 - here.c
+        self.depth = depth
+
+    def rows(self, at, start, parts):
+        size = self.depth // parts
+        return pl.ds(pl.multiple_of(at * self.depth + start * size, 16), size)
+
+    def y_half(self, at):
+        return self.rows(at, self.here.yy, 2)
+
+    def quarter(self, at, which):
+        return self.rows(at, 2 * self.here.yy + which, 4)
+
+    def send(self, where, device, lands, index=None):
+        src = self.buf.at[self.mine, where]
+        land = self.buf.at[self.mine if index is None else index, lands]
+        return self.links.move(src, src, device, land).start()
+
+    def issue(self):
+        here = self.here
+        for made in self.placed:
+            made.wait()
+        own = self.y_half(here.w)
+        self.from_left = self.send(own, here.to_right, self.y_half(here.left))
+        self.from_right = self.send(own, here.to_left, self.y_half(here.right))
+
+    def to_y(self, at):
+        return self.send(self.y_half(at), self.here.to_y, self.rows(at, 1 - self.here.yy, 2))
+
+    def forward(self):
+        here = self.here
+        self.from_left.landed()
+        self.far_top = self.send(self.quarter(here.left, 0), here.to_right, self.quarter(here.far, 0))
+        self.over_y = [self.to_y(here.left)]
+        self.from_right.landed()
+        self.far_low = self.send(self.quarter(here.right, 1), here.to_left, self.quarter(here.far, 1))
+        self.over_y.append(self.to_y(here.right))
+
+    def complete(self):
+        self.far_top.landed()
+        self.far_low.landed()
+        self.over_y.append(self.to_y(self.here.far))
+
+    def share(self):
+        here = self.here
+        self.cores = []
+        for made, at in zip(self.over_y, (here.left, here.right, here.far)):
+            made.landed()
+            whole = self.rows(at, 0, 1)
+            self.cores.append(self.send(whole, here.to_core, whole, self.other))
+
+    def ready(self):
+        for made in self.cores:
+            made.landed()
+
+
+def forward_kernel(
+    count, x_ref, mem_ref, map_ref, len_ref, gs_ref, gc_ref, gf_ref, ge_ref,
+    q_in, k_in, v_in, so_in, cq_in, ck_in, cv_in, co_in, ga_in, up_in, dn_in,
+    block_o, one_o, two_o, three_o, exit_o, q_o, k_o, v_o, cq_o, mk_o, mv_o, sc_o, cc_o, ps_o, pc_o,
+    ga_o, up_o, sel_o, wa_o, wgu_o, wd_o, gain_o,
+    wa, wgu, wd, gains, slots, packed, part_out, part_in, valid_slot,
+    block, one, two, three, exit_rows, q, k, v, cq, mk, mv, sc, cc, ps, pc, ga, up, gain_sum,
+    send_sems, recv_sems, copy_sems,
+):
+    here = position(count)
+    g, w, t = here.g, here.w, here.t
+    left, right, far = here.left, here.right, here.far
+    to_left, to_right, to_far, to_tp = here.to_left, here.to_right, here.to_far, here.to_tp
+    rows = x_ref.shape[0]
+    links, copies = Links(send_sems, recv_sems), Copies(copy_sems)
+    depth = q_in.shape[0]
+    wide_cols = dn_in.shape[1] // 2
+
+    own = pl.ds(pl.multiple_of(w * depth, 16), depth)
+    order = (q_in, k_in, v_in, so_in, ck_in, cv_in, cq_in, co_in)
+    weights = []
+    for j in range(4):
+        placed = [copies.start(order[2 * j + e], wa.at[2 * j + e, own]) for e in range(2)]
+        weights.append(Gather(here, links, wa, 2 * j, depth, placed))
+    placed = [copies.start(ref, wgu.at[e, own]) for e, ref in enumerate((ga_in, up_in))]
+    weights.append(Gather(here, links, wgu, 0, depth, placed))
+    placed = [copies.start(dn_in.at[:, pl.ds(e * wide_cols, wide_cols)], wd.at[e, own]) for e in range(2)]
+    weights.append(Gather(here, links, wd, 0, depth, placed))
+
+    gain_sum[...] = jnp.zeros_like(gain_sum)
+    for n, ref in enumerate((gs_ref, gc_ref, gf_ref, ge_ref)):
+        gain_sum[n : n + 1, 0:depth] = ref[...].astype(F32)
+    gains[w] = pltpu.roll(gain_sum[...], w * depth, 1)
+    greet([to_left, to_right, to_far, here.to_core, here.to_y, to_tp])
+    gain_moves = [
+        links.move(gains.at[w], gains.at[w], device, gains.at[at]).start()
+        for device, at in ((to_left, right), (to_right, left), (to_far, far))
+    ]
+    weights[0].issue()
+    weights[1].issue()
+
+    capacity = slots.shape[0] // count
+    choose = slot_choice(map_ref[:, pl.ds(pl.multiple_of(w * rows, rows), rows)], slots.shape[0], count)
+    packed[...] = dot_nn(choose, mem_ref[...]).astype(BF)
+
+    def slot_rows(at, which):
+        return pl.ds(pl.multiple_of(at * capacity + which * (capacity // 2), 16), capacity // 2)
+
+    slot_moves = [
+        links.move(packed.at[slot_rows(to, t)], slots.at[slot_rows(w, t)], device, slots.at[slot_rows(at, t)]).start()
+        for device, to, at in ((to_left, left, right), (to_right, right, left), (to_far, far, far))
+    ]
+    own_slots = pl.ds(pl.multiple_of(w * capacity, 16), capacity)
+    slots[own_slots, :] = packed[own_slots, :]
+    weights[0].forward()
+    weights[2].issue()
+
+    for made in gain_moves:
+        made.landed()
+    total_gain = gains[0]
+    for at in range(1, count):
+        total_gain = total_gain + gains[at]
+    gain_sum[...] = total_gain
+    hidden = x_ref[...].astype(F32)
+    norm_self = rms_rows(hidden, gain_sum[0:1, :])
+    weights[1].forward()
+    weights[0].complete()
+    weights[3].issue()
+    weights[0].share()
+    weights[1].complete()
+    weights[2].forward()
+    weights[1].share()
+    weights[4].issue()
+    weights[0].ready()
+    q[...] = dot_nn(norm_self, wa[0]).astype(BF)
+    k[...] = dot_nn(norm_self, wa[1]).astype(BF)
+    weights[2].complete()
+    weights[1].ready()
+    v[...] = dot_nn(norm_self, wa[2]).astype(BF)
+    slot_fills = []
+    for made, at in zip(slot_moves, (right, left, far)):
+        made.landed()
+        src = slots.at[slot_rows(at, t)]
+        slot_fills.append(links.move(src, src, to_tp, slots.at[slot_rows(at, 1 - t)]).start())
+    weights[3].forward()
+    length = len_ref[g * count + w]
+    query_at = lax.broadcasted_iota(jnp.int32, (2 * rows, rows), 0)
+    query_at = jnp.where(query_at >= rows, query_at - rows, query_at)
+    key_at = lax.broadcasted_iota(jnp.int32, (2 * rows, rows), 1)
+    allowed_self = (key_at <= query_at) & (key_at < length)
+    pairs = q.shape[1] // (2 * HEAD_DIM)
+    attention_forward(pairs, q, k, v, ps, sc, allowed_self)
+
+    def exchange_start(n):
+        return links.move(part_out.at[n], part_in.at[n], to_tp, part_in.at[n]).start()
+
+    def exchanged(n, made):
+        made.landed()
+        return part_out[n].astype(F32) + part_in[n].astype(F32)
+
+    part_out[0] = dot_nt(sc[...], wa[3]).astype(BF)
+    swap = exchange_start(0)
+    weights[2].share()
+    weights[5].issue()
+    weights[3].complete()
+    for made in slot_fills:
+        made.landed()
+    weights[3].share()
+    place = lax.broadcasted_iota(jnp.int32, (1, capacity), 1).astype(F32)
+    for b in range(count):
+        reads = jnp.sum(jnp.where(map_ref[:, b * rows : (b + 1) * rows] == w, 1.0, 0.0), axis=1, keepdims=True)
+        valid_slot[0:1, b * capacity : (b + 1) * capacity] = jnp.where(place < reads, 1.0, 0.0)
+    weights[2].ready()
+    mk[...] = dot_nn(slots[...], wa[4]).astype(BF)
+    mv[...] = dot_nn(slots[...], wa[5]).astype(BF)
+    weights[4].forward()
+    allowed_cross = jnp.broadcast_to(valid_slot[0:1, :], (2 * rows, slots.shape[0])) > 0.5
+    one[...] = hidden + exchanged(0, swap)
+    norm_cross = rms_rows(one[...], gain_sum[1:2, :])
+    weights[3].ready()
+    cq[...] = dot_nn(norm_cross, wa[6]).astype(BF)
+    weights[4].complete()
+    attention_forward(pairs, cq, mk, mv, pc, cc, allowed_cross)
+    part_out[1] = dot_nt(cc[...], wa[7]).astype(BF)
+    swap = exchange_start(1)
+    weights[4].share()
+    weights[5].forward()
+    weights[5].complete()
+    weights[5].share()
+    copies.save(wa, wa_o)
+    for src, dst in (
+        (q, q_o), (k, k_o), (v, v_o), (sc, sc_o), (ps, ps_o), (mk, mk_o), (mv, mv_o), (cq, cq_o), (cc, cc_o), (pc, pc_o),
+        (slots, sel_o), (one, one_o), (gain_sum, gain_o),
+    ):
+        copies.save(src, dst)
+    two[...] = one[...] + exchanged(1, swap)
+    copies.save(two, two_o)
+    norm_ff = rms_rows(two[...], gain_sum[2:3, :])
+    weights[4].ready()
+    copies.save(wgu, wgu_o)
+    ga[...] = dot_nn(norm_ff, wgu[0]).astype(BF)
+    up[...] = dot_nn(norm_ff, wgu[1]).astype(BF)
+    copies.save(ga, ga_o)
+    copies.save(up, up_o)
+    ff_hidden = (smooth_gate(ga[...].astype(F32)) * up[...].astype(F32)).astype(BF)
+    weights[5].ready()
+    copies.save(wd, wd_o)
+    part_out[2] = (
+        dot_nt(ff_hidden[:, :wide_cols], wd[0]) + dot_nt(ff_hidden[:, wide_cols:], wd[1])
+    ).astype(BF)
+    swap = exchange_start(2)
+    three[...] = two[...] + exchanged(2, swap)
+    block[...] = three[...].astype(BF)
+    exit_rows[...] = rms_rows(three[...], gain_sum[3:4, :])
+    copies.save(three, three_o)
+    copies.save(block, block_o)
+    copies.save(exit_rows, exit_o)
+    links.finish()
+    copies.finish()
+
+
+def forward_layer(count, layer_input, memory, group_map, lengths, gain_parts, weights):
+    rows, width = layer_input.shape
+    heads = weights[0].shape[1]
+    units = weights[8].shape[1]
+    slots = count * max(2, 2 * rows // count)
+    pairs = heads // (2 * HEAD_DIM)
+    kept = [
+        ((rows, width), BF), ((rows, width), F32), ((rows, width), F32), ((rows, width), F32), ((rows, width), BF),
+        ((rows, heads), BF), ((rows, heads), BF), ((rows, heads), BF), ((rows, heads), BF),
+        ((slots, heads), BF), ((slots, heads), BF), ((rows, heads), BF), ((rows, heads), BF),
+        ((pairs, 2 * rows, rows), BF), ((pairs, 2 * rows, slots), BF),
+        ((rows, units), BF), ((rows, units), BF), ((slots, width), BF),
+        ((8, width, heads), BF), ((2, width, units), BF), ((2, width, units // 2), BF), ((8, width), F32),
+    ]
+    vmem, hbm = pl.BlockSpec(memory_space=pltpu.VMEM), pl.BlockSpec(memory_space=pl.ANY)
+    scratch = [
+        pltpu.VMEM((8, width, heads), BF), pltpu.VMEM((2, width, units), BF), pltpu.VMEM((2, width, units // 2), BF),
+        pltpu.VMEM((count, 8, width), F32), pltpu.VMEM((slots, width), BF), pltpu.VMEM((slots, width), BF),
+        pltpu.VMEM((3, rows, width), BF), pltpu.VMEM((3, rows, width), BF), pltpu.VMEM((8, slots), F32),
+    ]
+    scratch += [pltpu.VMEM(shape, kind) for shape, kind in kept[:17]]
+    scratch += [pltpu.VMEM((8, width), F32)]
+    scratch += [pltpu.SemaphoreType.DMA((80,)), pltpu.SemaphoreType.DMA((80,)), pltpu.SemaphoreType.DMA((40,))]
+    return pl.pallas_call(
+        functools.partial(forward_kernel, count),
+        out_shape=[jax.ShapeDtypeStruct(shape, kind) for shape, kind in kept],
+        in_specs=[vmem, vmem, vmem, pl.BlockSpec(memory_space=pltpu.SMEM)] + [vmem] * 4 + [hbm] * 11,
+        out_specs=[hbm] * len(kept),
+        scratch_shapes=scratch,
+        compiler_params=pltpu.CompilerParams(
+            collective_id=0, has_side_effects=True, vmem_limit_bytes=VMEM_BYTES
+        ),
+        name="forward_layer",
+    )(layer_input, memory, group_map, lengths, *gain_parts, *weights)
+
+
+CHUNK = 512
+
+
+def tall(rows):
+    return -(-rows // (2 * CHUNK)) * 2 * CHUNK
+
+
+def span(at, size):
+    return pl.ds(pl.multiple_of(at * size, size), size)
+
+
+def exit_phase(here, links, rows_own, tab, tabt, gt, rb, ids, lens, high, total, stats, stats_tp, stats_wide, coef, weight, acc,
+               dx, land_far, land_near, swap_out, swap_in, grad_out, vocab, fillers):
+    count, g, w, t = here.count, here.g, here.w, here.t
+    left, right, far = here.left, here.right, here.far
+    to_left, to_right, to_far, to_tp = here.to_left, here.to_right, here.to_far, here.to_tp
+    rows, width = rows_own.shape
+    half = rows // 2
+    chunks = tab.shape[0] // CHUNK
+    scale = float(width) ** (-0.5)
+    base = (w * 2 + t) * vocab
+    tokens = count * rows
+
+    def block(b):
+        return span(b, rows)
+
+    def halved(b, which):
+        return pl.ds(pl.multiple_of(b * rows + which * half, half), half)
+
+    rb[block(w), :] = rows_own[...]
+    src = rb.at[block(w)]
+    from_left = links.move(src, src, to_right, rb.at[block(left)]).start()
+    from_right = links.move(src, src, to_left, rb.at[block(right)]).start()
+
+    def target_row(cols):
+        row = ids[:, cols] - base
+        return jnp.where(row < vocab, row, -1)
+
+    def flip(j, carry):
+        tabt[:, span(j, CHUNK)] = tab[span(j, CHUNK), :].T
+        return carry
+
+    def score(b):
+        cols = block(b)
+        wanted = target_row(cols)
+        block_rows = rb[cols, :]
+
+        def step(j, pick):
+            at = lax.broadcasted_iota(jnp.int32, (CHUNK, rows), 0) + j * CHUNK
+            logits = dot_nt(tab[span(j, CHUNK), :], block_rows) * scale
+            logits = jnp.where(at < vocab, logits, MASKED)
+            top = jnp.max(logits, axis=0, keepdims=True)
+            exponent = jnp.exp(logits - top)
+            high[pl.ds(j, 1), cols] = top
+            total[pl.ds(j, 1), cols] = jnp.sum(exponent, axis=0, keepdims=True)
+            gt[span(j, CHUNK), cols] = exponent.astype(BF)
+            return pick + jnp.sum(jnp.where(at == wanted, logits, 0.0), axis=0, keepdims=True)
+
+        pick = lax.fori_loop(0, chunks, step, jnp.zeros((1, rows), F32), unroll=True)
+        tops = high[:, cols]
+        top = jnp.max(tops, axis=0, keepdims=True)
+        stats[0:1, cols] = top
+        stats[1:2, cols] = jnp.sum(total[:, cols] * jnp.exp(tops - top), axis=0, keepdims=True)
+        stats[2:3, cols] = pick
+
+    score(w)
+    from_left.landed()
+    src = rb.at[halved(left, 0)]
+    far_top = links.move(src, src, to_right, rb.at[halved(far, 0)]).start()
+    from_right.landed()
+    src = rb.at[halved(right, 1)]
+    far_low = links.move(src, src, to_left, rb.at[halved(far, 1)]).start()
+    score(left)
+    score(right)
+    far_top.landed()
+    far_low.landed()
+    score(far)
+
+    def merged_stats(parts):
+        top = parts[0][0:1]
+        for part in parts[1:]:
+            top = jnp.maximum(top, part[0:1])
+        mass = sum(part[1:2] * jnp.exp(part[0:1] - top) for part in parts)
+        pick = sum(part[2:3] for part in parts)
+        return top, mass, pick
+
+    swap = links.move(stats, stats_tp, to_tp, stats_tp).start()
+    lax.fori_loop(0, chunks, flip, 0)
+    lengths = [lens[k] for k in range(lens.shape[0])]
+    tokens_all = lengths[0]
+    for length in lengths[1:]:
+        tokens_all = tokens_all + length
+    place = lax.broadcasted_iota(jnp.int32, (1, rows), 1)
+    for b in range(count):
+        inside = jnp.where(place < lens[g * count + b], 1.0, 0.0).astype(F32)
+        weight[0:1, b * rows : (b + 1) * rows] = inside / tokens_all.astype(F32)
+    swap.landed()
+    mine, other = stats[...], stats_tp[...]
+    top, mass, pick = merged_stats([mine, other])
+    joint = stats_wide.at[w]
+    joint[0:1, :] = top
+    joint[1:2, :] = mass
+    joint[2:3, :] = pick
+    spreads = [
+        links.move(joint, joint, device, stats_wide.at[at]).start()
+        for device, at in ((to_left, right), (to_right, left), (to_far, far))
+    ]
+    for made in spreads:
+        made.landed()
+    top, mass, pick = merged_stats([stats_wide[b] for b in range(count)])
+    log_total = top + jnp.log(mass)
+    all_weight = weight[0:1, :]
+    coef[...] = jnp.exp(high[...] - log_total) * all_weight
+    stats_tp[3:4, :] = (log_total - pick) * all_weight
+    loss = jnp.sum(stats_tp[3:4, block(w)], axis=1, keepdims=True)
+
+    def row_grads(b):
+        cols = block(b)
+        wanted = target_row(cols)
+        own_weight = weight[0:1, cols]
+        acc[...] = jnp.zeros_like(acc)
+
+        def step(j, carry):
+            at = lax.broadcasted_iota(jnp.int32, (CHUNK, rows), 0) + j * CHUNK
+            grad = gt[span(j, CHUNK), cols].astype(F32) * coef[pl.ds(j, 1), cols]
+            grad = (grad - jnp.where(at == wanted, own_weight, 0.0)).astype(BF)
+            gt[span(j, CHUNK), cols] = grad
+            acc[...] += dot_nn(tabt[:, span(j, CHUNK)], grad)
+            return carry
+
+        lax.fori_loop(0, chunks, step, 0, unroll=True)
+        return (acc[...] * scale).astype(BF).T
+
+    dx[0] = row_grads(far)
+    right_far = links.move(dx.at[0, pl.ds(0, half)], land_far.at[0], to_right, land_far.at[0]).start()
+    left_far = links.move(dx.at[0, pl.ds(half, half)], land_far.at[1], to_left, land_far.at[1]).start()
+    top_rows, low_rows = pl.ds(0, half), pl.ds(half, half)
+
+    def near(slot, where, side, device):
+        return links.move(dx.at[slot, where], land_near.at[side, where], device, land_near.at[side, where]).start()
+
+    dx[1] = row_grads(right)
+    right_low = near(1, low_rows, 0, to_right)
+    dx[2] = row_grads(left)
+    left_top = near(2, top_rows, 1, to_left)
+    right_far.landed()
+    dx[1, top_rows] = (dx[1, top_rows].astype(F32) + land_far[0].astype(F32)).astype(BF)
+    right_top = near(1, top_rows, 0, to_right)
+    left_far.landed()
+    dx[2, low_rows] = (dx[2, low_rows].astype(F32) + land_far[1].astype(F32)).astype(BF)
+    left_low = near(2, low_rows, 1, to_left)
+    dx[3] = row_grads(w)
+    fillers[0]()
+    swaps = []
+    for where, one_side, other_side in ((top_rows, left_top, right_top), (low_rows, right_low, left_low)):
+        one_side.landed()
+        other_side.landed()
+        joined = dx[3, where].astype(F32) + land_near[0, where].astype(F32) + land_near[1, where].astype(F32)
+        swap_out[where, :] = joined.astype(BF)
+        swaps.append(links.move(swap_out.at[where], swap_in.at[where], to_tp, swap_in.at[where]).start())
+    fillers[1]()
+    for made in swaps:
+        made.landed()
+    grad_out[...] = swap_out[...].astype(F32) + swap_in[...].astype(F32)
+    return loss
+
+
+class TableGrad:
+    def __init__(self, here, links, copies, tab, gt, rb, land_core, out):
+        self.here, self.links, self.copies = here, links, copies
+        self.tab, self.gt, self.rb, self.land_core, self.out = tab, gt, rb, land_core, out
+        self.pieces = tab.shape[0] // (2 * CHUNK)
+        self.scale = float(tab.shape[1]) ** (-0.5)
+        self.cores = []
+
+    def rows(self, owner, i):
+        return pl.ds(pl.multiple_of((owner * self.pieces + i) * CHUNK, CHUNK), CHUNK)
+
+    def product(self, where):
+        return dot_nn(self.gt[where, :], self.rb[...]) * self.scale
+
+    def first_half(self):
+        c = self.here.c
+        for i in range(self.pieces):
+            where = self.rows(1 - c, i)
+            self.tab[where, :] = self.product(where).astype(BF)
+            land = self.land_core.at[pl.ds(i * CHUNK, CHUNK)]
+            self.cores.append(self.links.move(self.tab.at[where], land, self.here.to_core, land).start())
+
+    def second_half(self):
+        c = self.here.c
+        for i in range(self.pieces):
+            where = self.rows(c, i)
+            mine = self.product(where)
+            self.cores[i].landed()
+            self.tab[where, :] = (mine + self.land_core[i * CHUNK : (i + 1) * CHUNK, :].astype(F32)).astype(BF)
+            self.copies.save(self.tab.at[where], self.out.at[pl.ds(i * CHUNK, CHUNK)])
+
+
+def exit_kernel(
+    count, vocab, rows_own, ids, lens, table, grad_o, loss_o, half_o,
+    tab, tabt, gt, rb, high, total, stats, stats_tp, stats_wide, coef, weight, acc, dx, land_far, land_near, swap_out, swap_in,
+    land_core, send_sems, recv_sems, copy_sems,
+):
+    here = position(count)
+    links, copies = Links(send_sems, recv_sems), Copies(copy_sems)
+    load = copies.start(table, tab.at[pl.ds(0, vocab)])
+    greet([here.to_left, here.to_right, here.to_far, here.to_core, here.to_tp])
+    tab[vocab:, :] = jnp.zeros((tab.shape[0] - vocab, tab.shape[1]), BF)
+    load.wait()
+    grads = TableGrad(here, links, copies, tab, gt, rb, land_core, half_o)
+    loss = exit_phase(here, links, rows_own, tab, tabt, gt, rb, ids, lens, high, total, stats, stats_tp, stats_wide, coef, weight,
+                      acc, dx, land_far, land_near, swap_out, swap_in, grad_o, vocab, (grads.first_half, grads.second_half))
+    loss_o[...] = jnp.broadcast_to(loss, loss_o.shape)
+    links.finish()
+    copies.finish()
+
+
+def exit_head(count, norm_exit, ids, lengths, table):
+    vocab, width = table.shape
+    rows = norm_exit.shape[0]
+    high = tall(vocab)
+    chunks = high // CHUNK
+    tokens = rows * count
+    vmem, hbm = pl.BlockSpec(memory_space=pltpu.VMEM), pl.BlockSpec(memory_space=pl.ANY)
+    return pl.pallas_call(
+        functools.partial(exit_kernel, count, vocab),
+        out_shape=[
+            jax.ShapeDtypeStruct((rows, width), F32), jax.ShapeDtypeStruct((8, 128), F32),
+            jax.ShapeDtypeStruct((high // 2, width), BF),
+        ],
+        in_specs=[vmem, vmem, pl.BlockSpec(memory_space=pltpu.SMEM), hbm],
+        out_specs=[vmem, vmem, hbm],
+        scratch_shapes=[
+            pltpu.VMEM((high, width), BF), pltpu.VMEM((width, high), BF), pltpu.VMEM((high, tokens), BF),
+            pltpu.VMEM((tokens, width), BF), pltpu.VMEM((chunks, tokens), F32), pltpu.VMEM((chunks, tokens), F32),
+            pltpu.VMEM((8, tokens), F32), pltpu.VMEM((8, tokens), F32), pltpu.VMEM((count, 8, tokens), F32),
+            pltpu.VMEM((chunks, tokens), F32), pltpu.VMEM((8, tokens), F32), pltpu.VMEM((width, rows), F32),
+            pltpu.VMEM((4, rows, width), BF), pltpu.VMEM((2, rows // 2, width), BF), pltpu.VMEM((2, rows, width), BF),
+            pltpu.VMEM((rows, width), BF), pltpu.VMEM((rows, width), BF),
+            pltpu.VMEM((high // 2, width), BF),
+            pltpu.SemaphoreType.DMA((40,)), pltpu.SemaphoreType.DMA((40,)), pltpu.SemaphoreType.DMA((16,)),
+        ],
+        compiler_params=pltpu.CompilerParams(
+            collective_id=1, has_side_effects=True, vmem_limit_bytes=VMEM_BYTES
+        ),
+        name="exit_head",
+    )(norm_exit, ids, lengths, table)
+
+
+GELU_SCALE = 0.7978845608028654
+GELU_CUBE = 0.044715
+
+
+def norm_back(values, gain, grad):
+    factor = lax.rsqrt(jnp.mean(values * values, axis=1, keepdims=True) + EPSILON)
+    unit = values * factor
+    scaled = grad * gain
+    inner = jnp.mean(scaled * values, axis=1, keepdims=True)
+    return jnp.sum(grad * unit, axis=0, keepdims=True), factor * scaled - unit * (factor * factor * inner)
+
+
+def attention_backward(pairs, queries, keys, values, probs, context_grad, query_grad, key_grad, value_grad):
+    factor = HEAD_DIM ** (-0.5)
+
+    def step(p, carry):
+        cols = pair_columns(p)
+        grad = both_heads(context_grad[:, cols])
+        soft = probs[p]
+        soft_float = soft.astype(F32)
+        soft_grad = dot_nt(grad, values[:, cols])
+        inner = jnp.sum(soft_float * soft_grad, axis=1, keepdims=True)
+        score_grad = (soft_float * (soft_grad - inner)).astype(BF)
+        query_grad[:, cols] = (pick_heads(dot_nn(score_grad, keys[:, cols])) * factor).astype(BF)
+        key_grad[:, cols] = (dot_tn(score_grad, both_heads(queries[:, cols])) * factor).astype(BF)
+        value_grad[:, cols] = dot_tn(soft, grad).astype(BF)
+        return carry
+
+    lax.fori_loop(0, pairs, step, 0)
+
+
+class WeightGrad:
+    def __init__(self, here, links, copies, grads, first, depth, land_core, land_far, land_near, land_y, mine_out, out):
+        self.here, self.links, self.copies = here, links, copies
+        self.grads, self.mine, self.other = grads, first + here.c, first + 1 - here.c
+        self.depth, self.half = depth, depth // 2
+        self.land_core, self.land_far, self.land_near, self.land_y = land_core, land_far, land_near, land_y
+        self.mine_out, self.out = mine_out, out
+
+    def whole(self, at):
+        return pl.ds(pl.multiple_of(at * self.depth, 16), self.depth)
+
+    def part(self, at, which):
+        return pl.ds(pl.multiple_of(at * self.depth + which * self.half, 16), self.half)
+
+    def pair(self):
+        self.core = self.links.move(
+            self.grads.at[self.other], self.land_core, self.here.to_core, self.land_core
+        ).start()
+
+    def near(self, where, side, which, device):
+        rows = pl.ds(which * self.half, self.half)
+        return self.links.move(
+            self.grads.at[self.mine, where], self.land_near.at[side, rows], device, self.land_near.at[side, rows]
+        ).start()
+
+    def add_core(self, where):
+        self.grads[self.mine, where] = (
+            self.grads[self.mine, where].astype(F32) + self.land_core[where].astype(F32)
+        ).astype(BF)
+
+    def ring(self):
+        here = self.here
+        self.core.landed()
+        for at in (here.far, here.right, here.left):
+            self.add_core(self.whole(at))
+            if at is here.far:
+                self.far = [
+                    self.links.move(
+                        self.grads.at[self.mine, self.part(at, e)], self.land_far.at[e], way, self.land_far.at[e]
+                    ).start()
+                    for e, way in enumerate((here.to_right, here.to_left))
+                ]
+        self.early = [
+            self.near(self.part(here.right, 1), 0, 1, here.to_right),
+            self.near(self.part(here.left, 0), 1, 0, here.to_left),
+        ]
+        self.add_core(self.whole(here.w))
+
+    def pass_on(self):
+        here = self.here
+        self.late = []
+        for e, side, way in ((0, here.right, here.to_right), (1, here.left, here.to_left)):
+            self.far[e].landed()
+            where = self.part(side, e)
+            self.grads[self.mine, where] = (
+                self.grads[self.mine, where].astype(F32) + self.land_far[e].astype(F32)
+            ).astype(BF)
+            self.late.append(self.near(where, e, e, way))
+
+    def across(self):
+        for made in self.early + self.late:
+            made.landed()
+        where = self.whole(self.here.w)
+        self.mine_out[0] = (
+            self.grads[self.mine, where].astype(F32) + self.land_near[0].astype(F32) + self.land_near[1].astype(F32)
+        ).astype(BF)
+        self.y = self.links.move(self.mine_out.at[0], self.land_y, self.here.to_y, self.land_y).start()
+
+    def settle(self):
+        self.y.landed()
+        self.mine_out[1] = (self.mine_out[0].astype(F32) + self.land_y[...].astype(F32)).astype(BF)
+        src = self.mine_out.at[1]
+        self.copies.save(src, self.out.at[self.mine])
+        self.share = self.links.move(
+            src, self.out.at[self.mine], self.here.to_core, self.out.at[self.other]
+        ).start()
+
+    def done(self):
+        self.share.landed()
+
+
+def backward_kernel(
+    count,
+    lens, map_ref, x_h, og_h, eg_h, loss_h, one_h, two_h, three_h, q_h, k_h, v_h, cq_h, mk_h, mv_h, sc_h, cc_h, ps_h, pc_h,
+    ga_h, up_h, sel_h, wa_h, wgu_h, wd_h, gain_h, half_h,
+    in_o, mem_o, small_o, ga8_o, ggu_o, gd_o, table_o,
+    x, og, eg, loss, one, two, three, q, k, v, cq, mk, mv, sc, cc, ps, pc, ga, up, sel, wa, wgu, wd, gain, tab, land_t,
+    part_out, part_in, grad, dq, dk, dv, dmk, dmv, dctx, gate_grad, up_grad, ff_hidden,
+    g8, ggu, gd, lc8, lcg, lcd, lf8, lfg, lfd, ln8, lng, lnd, ly8, lyg, lyd, mo8, mog, mod,
+    back_slots, got_slots, small, small_wide, small_land,
+    send_sems, recv_sems, copy_sems,
+):
+    here = position(count)
+    links, copies = Links(send_sems, recv_sems), Copies(copy_sems)
+    g, w, c = here.g, here.w, here.c
+    to_left, to_right, to_far, to_tp = (here.to_left, here.to_right, here.to_far, here.to_tp)
+    loads = {}
+    for src, dst in (
+        (gain_h, gain), (three_h, three), (eg_h, eg), (og_h, og), (ga_h, ga), (up_h, up), (wd_h, wd), (half_h, tab), (wgu_h, wgu),
+        (two_h, two), (wa_h, wa), (cc_h, cc), (pc_h, pc), (cq_h, cq), (mk_h, mk), (mv_h, mv), (sel_h, sel), (one_h, one),
+        (sc_h, sc), (ps_h, ps), (q_h, q), (k_h, k), (v_h, v), (x_h, x), (loss_h, loss),
+    ):
+        loads[id(dst)] = copies.start(src, dst)
+
+    def need(*refs):
+        for ref in refs:
+            loads.pop(id(ref)).wait()
+
+    greet([to_left, to_right, to_far, here.to_core, here.to_y, to_tp])
+
+    pieces = tab.shape[0] // CHUNK
+    need(tab)
+    crossing = [
+        links.move(tab.at[pl.ds(i * CHUNK, CHUNK)], land_t.at[pl.ds(i * CHUNK, CHUNK)], here.to_y, land_t.at[pl.ds(i * CHUNK, CHUNK)]).start()
+        for i in range(pieces)
+    ]
+    shares = []
+
+    def settle_table(i):
+        piece = pl.ds(i * CHUNK, CHUNK)
+        crossing[i].landed()
+        crossing[i].sent()
+        tab[piece, :] = (tab[piece, :].astype(F32) + land_t[piece, :].astype(F32)).astype(BF)
+
+        def rows(owner):
+            return pl.ds(pl.multiple_of((owner * pieces + i) * CHUNK, CHUNK), CHUNK)
+
+        copies.save(tab.at[piece], table_o.at[rows(c)])
+        shares.append(
+            links.move(tab.at[piece], table_o.at[rows(c)], here.to_core, table_o.at[rows(1 - c)]).start()
+        )
+
+    depth = g8.shape[1] // count
+
+    def weight_pair(i):
+        if i < 4:
+            return WeightGrad(here, links, copies, g8, 2 * i, depth, lc8.at[i], lf8.at[i], ln8.at[i], ly8.at[i], mo8.at[i], ga8_o)
+        if i == 4:
+            return WeightGrad(here, links, copies, ggu, 0, depth, lcg, lfg, lng, lyg, mog, ggu_o)
+        return WeightGrad(here, links, copies, gd, 0, depth, lcd, lfd, lnd, lyd, mod, gd_o)
+
+    pair = [weight_pair(i) for i in range(6)]
+
+    def exchange_start(n):
+        return links.move(part_out.at[n], part_in.at[n], to_tp, part_in.at[n]).start()
+
+    def exchanged(n, made):
+        made.landed()
+        return part_out[n].astype(F32) + part_in[n].astype(F32)
+
+    small[...] = jnp.zeros_like(small)
+    need(gain, three, eg, og)
+    gain_row, back = norm_back(three[...], gain[3:4, :], eg[...])
+    small[3:4, :] = gain_row
+    grad[...] = og[...].astype(F32) + back
+    branch = grad[...].astype(BF)
+    need(ga, up, wd)
+    units = wd.shape[2]
+    for e in range(2):
+        cols = slice(e * units, (e + 1) * units)
+        act = ga[:, cols].astype(F32)
+        up_act = up[:, cols].astype(F32)
+        square = act * act
+        bend = jnp.tanh(GELU_SCALE * (act + GELU_CUBE * act * square))
+        gate = 0.5 * act * (1.0 + bend)
+        slope = 0.5 * (1.0 + bend) + 0.5 * act * (1.0 - bend * bend) * (GELU_SCALE * (1.0 + 3.0 * GELU_CUBE * square))
+        hidden_grad = dot_nn(branch, wd[e])
+        gate_grad[:, cols] = (hidden_grad * up_act * slope).astype(BF)
+        up_grad[:, cols] = (hidden_grad * gate).astype(BF)
+        ff_hidden[:, cols] = (gate * up_act).astype(BF)
+    need(wgu)
+    part_out[0] = (dot_nt(gate_grad[...], wgu[0]) + dot_nt(up_grad[...], wgu[1])).astype(BF)
+    swap = exchange_start(0)
+    need(two)
+    norm_t = rms_rows(two[...], gain[2:3, :]).T
+    ggu[0] = dot_nn(norm_t, gate_grad[...]).astype(BF)
+    ggu[1] = dot_nn(norm_t, up_grad[...]).astype(BF)
+    pair[4].pair()
+    branch_rows = branch.T
+    for e in range(2):
+        gd[e] = dot_nn(branch_rows, ff_hidden[:, e * units : (e + 1) * units]).astype(BF)
+    pair[5].pair()
+    pair[4].ring()
+    gain_row, back = norm_back(two[...], gain[2:3, :], exchanged(0, swap))
+    small[2:3, :] = gain_row
+    grad[...] += back
+
+    branch = grad[...].astype(BF)
+    need(wa, cc, pc, cq, mk, mv, sel)
+    dctx[...] = dot_nn(branch, wa[7]).astype(BF)
+    pairs = dctx.shape[1] // (2 * HEAD_DIM)
+    attention_backward(pairs, cq, mk, mv, pc, dctx, dq, dmk, dmv)
+    part_out[1] = dot_nt(dq[...], wa[6]).astype(BF)
+    swap = exchange_start(1)
+    pair[5].ring()
+    pair[4].pass_on()
+    need(one)
+    back_slots[...] = (dot_nt(dmk[...], wa[4]) + dot_nt(dmv[...], wa[5])).astype(BF)
+    capacity = back_slots.shape[0] // count
+
+    def slot_rows(at):
+        return pl.ds(pl.multiple_of(at * capacity, 16), capacity)
+
+    returns = [
+        links.move(back_slots.at[slot_rows(to)], got_slots.at[slot_rows(w)], device, got_slots.at[slot_rows(at)]).start()
+        for device, to, at in ((to_left, here.left, here.right), (to_right, here.right, here.left), (to_far, here.far, here.far))
+    ]
+    got_slots[slot_rows(w), :] = back_slots[slot_rows(w), :]
+    g8[7] = dot_nn(branch.T, cc[...]).astype(BF)
+    norm_t = rms_rows(one[...], gain[1:2, :]).T
+    g8[6] = dot_nn(norm_t, dq[...]).astype(BF)
+    pair[3].pair()
+    slots_t = sel[...].T
+    g8[4] = dot_nn(slots_t, dmk[...]).astype(BF)
+    g8[5] = dot_nn(slots_t, dmv[...]).astype(BF)
+    pair[2].pair()
+    pair[4].across()
+    pair[5].pass_on()
+    pair[3].ring()
+    pair[2].ring()
+    gain_row, back = norm_back(one[...], gain[1:2, :], exchanged(1, swap))
+    small[1:2, :] = gain_row
+    grad[...] += back
+
+    branch = grad[...].astype(BF)
+    need(sc, ps, q, k, v, x)
+    dctx[...] = dot_nn(branch, wa[3]).astype(BF)
+    attention_backward(pairs, q, k, v, ps, dctx, dq, dk, dv)
+    part_out[2] = (dot_nt(dq[...], wa[0]) + dot_nt(dk[...], wa[1]) + dot_nt(dv[...], wa[2])).astype(BF)
+    swap = exchange_start(2)
+    hidden = x[...].astype(F32)
+    norm_t = rms_rows(hidden, gain[0:1, :]).T
+    g8[0] = dot_nn(norm_t, dq[...]).astype(BF)
+    g8[1] = dot_nn(norm_t, dk[...]).astype(BF)
+    pair[0].pair()
+    g8[2] = dot_nn(norm_t, dv[...]).astype(BF)
+    g8[3] = dot_nn(branch.T, sc[...]).astype(BF)
+    pair[1].pair()
+    pair[3].pass_on()
+    pair[2].pass_on()
+    pair[5].across()
+    pair[0].ring()
+    pair[1].ring()
+    for made in returns:
+        made.landed()
+    rows = x.shape[0]
+    choose = slot_choice(map_ref[:, pl.ds(pl.multiple_of(w * rows, rows), rows)], got_slots.shape[0], count)
+    part_out[3] = dot_tn(choose, got_slots[...]).astype(BF)
+    memory_swap = exchange_start(3)
+    gain_row, back = norm_back(hidden, gain[0:1, :], exchanged(2, swap))
+    small[0:1, :] = gain_row
+    grad[...] += back
+    copies.save(grad, in_o)
+    need(loss)
+    small[4:5, 0:128] = loss[0:1, :]
+
+    small_wide[w] = small[...]
+    sums = [
+        links.move(small, small_wide.at[w], device, small_wide.at[at]).start()
+        for device, at in ((to_left, here.right), (to_right, here.left), (to_far, here.far))
+    ]
+    pair[0].pass_on()
+    pair[1].pass_on()
+    pair[3].across()
+    pair[2].across()
+    for made in sums:
+        made.landed()
+    total = small_wide[0]
+    for b in range(1, count):
+        total = total + small_wide[b]
+    for n, way in enumerate((here.to_core, here.to_y)):
+        small_land[2 * n] = total
+        made = links.move(small_land.at[2 * n], small_land.at[2 * n + 1], way, small_land.at[2 * n + 1]).start()
+        if n == 0:
+            pair[0].across()
+            pair[1].across()
+        made.landed()
+        total = total + small_land[2 * n + 1]
+    small_o[...] = total
+    mem_o[...] = exchanged(3, memory_swap)
+    for i in range(pieces):
+        settle_table(i)
+    for i in (4, 5, 3, 2, 0, 1):
+        pair[i].settle()
+    for i in (4, 5, 3, 2, 0, 1):
+        pair[i].done()
+    for made in shares:
+        made.landed()
+    links.finish_rest(crossing)
+    copies.finish()
+
+
+def backward_layer(count, lengths, group_map, kept, table_half):
+    (layer_input, out_grad, exit_rows_grad, loss_part, one, two, three, q, k, v, cq, mk, mv, sc, cc, ps, pc, ga, up, sel,
+     wa, wgu, wd, gains) = kept
+    rows, width = layer_input.shape
+    heads, units = wa.shape[2], ga.shape[1]
+    slots, depth = sel.shape[0], width // count
+    half, narrow = depth // 2, units // 2
+    piece_rows = table_half.shape[0]
+    high = 2 * piece_rows
+    vmem, hbm = pl.BlockSpec(memory_space=pltpu.VMEM), pl.BlockSpec(memory_space=pl.ANY)
+
+    def three_kinds(rows_of, lead=()):
+        return [
+            pltpu.VMEM((4,) + lead + (rows_of, heads), BF), pltpu.VMEM(lead + (rows_of, units), BF),
+            pltpu.VMEM(lead + (rows_of, narrow), BF),
+        ]
+
+    scratch = [pltpu.VMEM(value.shape, value.dtype) for value in kept]
+    scratch += [pltpu.VMEM((piece_rows, width), BF), pltpu.VMEM((piece_rows, width), BF)]
+    scratch += [
+        pltpu.VMEM((4, rows, width), BF), pltpu.VMEM((4, rows, width), BF), pltpu.VMEM((rows, width), F32),
+        pltpu.VMEM((rows, heads), BF), pltpu.VMEM((rows, heads), BF), pltpu.VMEM((rows, heads), BF),
+        pltpu.VMEM((slots, heads), BF), pltpu.VMEM((slots, heads), BF), pltpu.VMEM((rows, heads), BF),
+        pltpu.VMEM((rows, units), BF), pltpu.VMEM((rows, units), BF), pltpu.VMEM((rows, units), BF),
+        pltpu.VMEM((8, width, heads), BF), pltpu.VMEM((2, width, units), BF), pltpu.VMEM((2, width, narrow), BF),
+    ]
+    scratch += three_kinds(width)
+    scratch += three_kinds(half, (2,))
+    scratch += three_kinds(depth, (2,))
+    scratch += three_kinds(depth)
+    scratch += three_kinds(depth, (2,))
+    scratch += [
+        pltpu.VMEM((slots, width), BF), pltpu.VMEM((slots, width), BF), pltpu.VMEM((8, width), F32),
+        pltpu.VMEM((count, 8, width), F32), pltpu.VMEM((4, 8, width), F32),
+        pltpu.SemaphoreType.DMA((80,)), pltpu.SemaphoreType.DMA((80,)), pltpu.SemaphoreType.DMA((48,)),
+    ]
+    return pl.pallas_call(
+        functools.partial(backward_kernel, count),
+        out_shape=[
+            jax.ShapeDtypeStruct((rows, width), F32), jax.ShapeDtypeStruct((rows, width), F32),
+            jax.ShapeDtypeStruct((8, width), F32), jax.ShapeDtypeStruct((8, depth, heads), BF),
+            jax.ShapeDtypeStruct((2, depth, units), BF), jax.ShapeDtypeStruct((2, depth, narrow), BF),
+            jax.ShapeDtypeStruct((high, width), BF),
+        ],
+        in_specs=[pl.BlockSpec(memory_space=pltpu.SMEM), vmem] + [hbm] * (len(kept) + 1),
+        out_specs=[hbm, vmem, vmem, hbm, hbm, hbm, hbm],
+        scratch_shapes=scratch,
+        compiler_params=pltpu.CompilerParams(
+            collective_id=2, has_side_effects=True, vmem_limit_bytes=VMEM_BYTES
+        ),
+        name="backward_layer",
+    )(lengths, group_map, *kept, table_half)
+
+
+def fused_body(
+    layer_input,
+    memory,
+    reader_map,
+    target_ids,
+    target_lengths,
+    out_grad,
+    self_q,
+    self_k,
+    self_v,
+    self_o,
+    cross_q,
+    cross_k,
+    cross_v,
+    cross_o,
+    ff_gate,
+    ff_up,
+    ff_out,
+    gain_self,
+    gain_cross,
+    gain_ff,
+    gain_exit,
+    exit_table,
+):
+    count = lax.axis_size("wide")
+    wide_index = lax.axis_index("wide")
+    depth = gain_self.shape[0]
+    group_map = reader_map[None, :]
+    (
+        block_output, resid_one, resid_two, resid_three, norm_exit, queries, keys, values, cross_queries,
+        keys_read, values_read, context_self, context_cross, probs_self, probs_cross, gate_act, up_act, slots,
+        attn_weights, gate_weights, down_weights, gains,
+    ) = forward_layer(
+        count, layer_input, memory, group_map, target_lengths,
+        tuple(gain[None, :] for gain in (gain_self, gain_cross, gain_ff, gain_exit)),
+        (self_q, self_k, self_v, self_o, cross_q, cross_k, cross_v, cross_o, ff_gate, ff_up, ff_out),
+    )
+    exit_rows_grad, loss_part, table_half = exit_head(
+        count, norm_exit, target_ids[None, :], target_lengths, exit_table
+    )
+    input_grad, memory_grad, small, attn_grads, gate_grads, down_grads, table_grad = backward_layer(
+        count, target_lengths, group_map,
+        (
+            layer_input, out_grad, exit_rows_grad, loss_part, resid_one, resid_two, resid_three, queries, keys, values,
+            cross_queries, keys_read, values_read, context_self, context_cross, probs_self, probs_cross, gate_act, up_act,
+            slots, attn_weights, gate_weights, down_weights, gains,
+        ),
+        table_half,
+    )
+    own_gains = lax.dynamic_slice(small, (0, wide_index * depth), (4, depth))
+    attn = attn_grads.astype(jnp.float32)
+    gate = gate_grads.astype(jnp.float32)
+    down = jnp.concatenate([down_grads[0], down_grads[1]], axis=1).astype(jnp.float32)
+    return (
+        block_output, small[4, 0], input_grad, memory_grad, attn[0], attn[1], attn[2], attn[3], attn[6], attn[4], attn[5],
+        attn[7], gate[0], gate[1], down, own_gains[0], own_gains[1], own_gains[2], own_gains[3],
+        table_grad[: exit_table.shape[0]].astype(jnp.float32),
+    )
+
+
+def fits(mesh):
+    return mesh.shape["wide"] == 4 and mesh.shape["tp"] == 2 and mesh.shape["grp"] == 4
+
+
 def solution(mesh):
     placed = (
         P(("grp", "wide"), None),
@@ -464,7 +1570,7 @@
         P(("wide", "tp"), None),
     )
     return jax.shard_map(
-        body,
+        fused_body if fits(mesh) else plain_body,
         mesh=mesh,
         in_specs=placed,
         out_specs=(

time: 1320 us -> 325 us (0.25); the launches traced: 1300 us -> 320 us
  waiting for transfers between devices: 693 us -> 0 us
  Pallas kernels: 0 us -> 295 us
  blocking collectives: 219 us -> 0 us
  matrix products: 177 us -> 0 us
  other arithmetic: 124 us -> 11.1 us
  local copies, waits for them, and re-layouts: 64 us -> 13 us
  between operations: 21.4 us -> 0.95 us
    reduce_scatter x12 -> x0, waiting for transfers between devices: 303 us -> none  [the longest x1 51.7 us: body(): lax.psum_scatter(rows_grad_all.astype(jnp.bfloat16), 'wide', scatter_dime...]
    pallas_call x0 -> x3, Pallas kernels: none -> 295 us  [the longest x1 131 us: backward_layer(): pl.pallas_call(functools.partial(backward_kernel, count), out_shape=[jax....]
    psum x8 -> x0, waiting for transfers between devices: 283 us -> none  [the longest x1 137 us: body(): lax.psum(shards[5].astype(jnp.bfloat16), 'grp').astype(jnp.float32)]
    all_gather x13 -> x0, blocking collectives: 197 us -> none  [the longest x3 61.7 us: merged(): lax.all_gather(part.astype(kind), axis)]
    dot_general x120 -> x0, matrix products: 177 us -> none  [the longest x48 65.6 us: project_back(): lax.dot_general(left, right, (((1,), (1,)), ((), ())), preferred_element_...]
    all_gather x4 -> x0, waiting for transfers between devices: 105 us -> none  [the longest x1 35.2 us: body(): lax.all_gather(ff_out, 'wide', axis=0, tiled=True)]
    convert_element_type x55 -> x4, other arithmetic: 47.4 us -> 11.1 us  [the longest x1 8.56 us: fused_body(): table_grad[:exit_table.shape[0]].astype(jnp.float32)]
    lt x13 -> x0, other arithmetic: 31.5 us -> none  [the longest x12 30.3 us: read_slots(): place % capacity]
  transfers between devices with their start and end apart: 26 -> 0, of which waited for: 20 -> 0; matrix products, arithmetic and copies ran while one was open for 9% -> 0% of each run, Pallas kernels for 0% -> 0%
where the time goes in v2:
time: 325 us; the launch traced here: 320 us
  Pallas kernels  295 us (91%)
  local copies, waits for them, and re-layouts  13 us (4%)
  other arithmetic  11.1 us (3%)
    pallas_call x1, Pallas kernels, backward_layer(): pl.pallas_call(functools.partial(backward_kernel, count), out_shape=[jax....  131 us
    pallas_call x1, Pallas kernels, forward_layer(): pl.pallas_call(functools.partial(forward_kernel, count), out_shape=[jax.S...  86.8 us
    pallas_call x1, Pallas kernels, exit_head(): pl.pallas_call(functools.partial(exit_kernel, count, vocab), out_shape=[j...  77.2 us
    convert_element_type x1, other arithmetic, fused_body(): table_grad[:exit_table.shape[0]].astype(jnp.float32)  8.56 us

profile of v2, /device:TPU:19, one launch (start us, length us, event | category | flops | bytes accessed | tf_op | source)
XLA Modules:
  0.0 320.4 jit_solution(17455107834822915207)
XLA Ops:
  0.7 1.2 broadcast_in_dim.19.gs_ref
  1.9 1.2 broadcast_in_dim.20.gc_ref
  3.1 1.2 broadcast_in_dim.21.gf_ref
  4.3 1.2 broadcast_in_dim.22.ge_ref
  5.5 86.8 %forward_layer.1 = (bf16[256,768]{1,0:T(8,128)(2,1)}, f32[256,768]{1,0:T(8,128)}, f32[256,768]{1,0:T(8,128)}, f32[256,768]{1,0:T(8,128)}, bf16[256,768]{1,0:T(8,...) custom-call(bf16[256,768]{1,0:T(8,128)(2,1)} %x_h.1, ...), custom_call_target="tpu_custom_call" | custom-call | tf_op jit(solution)/shard_map/forward_layer/pallas_call | solution.py:843
  92.3 77.2 %exit_head.1 = (f32[256,768]{1,0:T(8,128)}, f32[8,128]{1,0:T(8,128)}, bf16[2048,768]{1,0:T(8,128)(2,1)}) custom-call(bf16[256,768]{1,0:T(8,128)(2,1)} %get-tuple-element.53.rows_own, s32[1,1024]{1,0:T(1,128)} %bitcast.33, s32[16]{0:T(128)} %lens.3, bf16[4016,768]{1,0:T(8,128)(2,1)} %table.1), custom_call_target="tpu_custom_call" | custom-call | tf_op jit(solution)/shard_map/exit_head/pallas_call | solution.py:1081
  169.6 131.4 %backward_layer.1 = (f32[256,768]{1,0:T(8,128)}, f32[256,768]{1,0:T(8,128)}, f32[8,768]{1,0:T(8,128)}, bf16[8,192,384]{2,1,0:T(8,128)(2,1)}, bf16[2,192,1024]{2,...) custom-call(s32[16]{0:T(128)} %lens.3, s32[1,1024]{1,0:T(1,128)} %bitcast.32, ...), custom_call_target="tpu_custom_call" | custom-call | tf_op jit(solution)/shard_map/backward_layer/pallas_call | solution.py:1465
  301.0 1.2 slice.54
  302.2 1.4 convert_element_type.12
  303.6 0.0 copy-start.2
  303.6 1.4 slice_bitcast_fusion.2
  305.0 0.0 copy-start.4
  305.0 0.2 copy-done.2
  305.2 0.2 convert_element_type.13
  305.4 1.2 slice_bitcast_fusion
  306.6 0.0 copy-done.4
  306.6 1.0 maximum_convert_fusion
  307.6 1.5 fusion
  309.1 0.0 copy-start.3
  309.1 0.0 copy-start.1
  309.1 0.0 copy-start
  309.1 8.6 %slice_convert_fusion = f32[4016,768]{1,0:T(8,128)} fusion(bf16[4096,768]{1,0:T(8,128)(2,1)} %get-tuple-element.83), kind=kLoop, calls=%fused_computation | loop fusion | flops 3084288 | bytes 18505728 | tf_op jit(solution)/shard_map/convert_element_type | solution.py:1539
  317.7 0.0 copy-done.3
  317.7 0.7 copy.45
  318.4 0.0 copy-done.1
  318.4 0.9 copy.46
  319.3 0.0 copy-done
  319.3 0.9 copy.47
  (1 shorter events, 0.0 us)
Async XLA Ops:
  303.6 1.6 copy-start.2
  305.0 1.6 copy-start.4
  309.1 8.6 %copy-start.3 = (bf16[256,768]{1,0:T(8,128)(2,1)S(1)}, bf16[256,768]{1,0:T(8,128)(2,1)}, u32[]{:S(2)}) copy-start(bf16[256,768]{1,0:T(8,128)(2,1)} %get-tuple-element.120) | copy-start | bytes 1179652
  309.1 9.3 %copy-start.1 = (f32[256,768]{1,0:T(8,128)S(1)}, f32[256,768]{1,0:T(8,128)}, u32[]{:S(2)}) copy-start(f32[256,768]{1,0:T(8,128)} %get-tuple-element.122) | copy-start | bytes 2359300
  309.1 10.2 %copy-start = (f32[256,768]{1,0:T(8,128)S(1)}, f32[256,768]{1,0:T(8,128)}, u32[]{:S(2)}) copy-start(f32[256,768]{1,0:T(8,128)} %get-tuple-element.123) | copy-start | bytes 2359300
